TPU v7x, 128 devices: a whole 4x4x4 slice. The times are simulated.
128 devices in a mesh: dp: 32 (over y_lo, z, x), mp: 4 (over y_hi, core).
Axes of the slice: x: 4, y: 4 (y_hi: 2, y_lo: 2; y = y_hi * 2 + y_lo), z: 4, core: 2. Of those that a mesh axis runs over, the one named last changes fastest.
Arguments:
- frames: bfloat16 [1536, 81, 512], P(('dp', 'mp')), may hold values from -6 to 6
- camera_ids: int32 [1536], P(('dp', 'mp')), may hold values from 0 to 1
- instruction_ids: int32 [256], P('dp'), may hold values from 0 to 743
- action_bins: int32 [1536, 11], P('dp'), may hold values from 0 to 255
- final_mask: int32 [1536], P('dp'), may hold values 0 or 1
- step_count: int32 [1], replicated, may hold values from 2 to 20
- conv_w: float32 [1033, 3072], P(None, ('dp', 'mp')), may hold values from -0.75 to 0.75
- conv_m1: float32 [1033, 3072], P(None, ('dp', 'mp')), may hold values from -4.7683716e-06 to 4.7683716e-06
- conv_m2: float32 [1033, 3072], P(None, ('dp', 'mp')), may hold values from 2.3060689e-14 to 1.8448551e-13
- cond_w: float32 [1770, 512], P(None, ('dp', 'mp')), may hold values from -0.75 to 0.75
- cond_m1: float32 [1770, 512], P(None, ('dp', 'mp')), may hold values from -4.7683716e-06 to 4.7683716e-06
- cond_m2: float32 [1770, 512], P(None, ('dp', 'mp')), may hold values from 2.3060689e-14 to 1.8448551e-13
- small_w: float32 [11, 512], P(None, ('dp', 'mp')), may hold values from -4 to 4
- small_m1: float32 [11, 512], P(None, ('dp', 'mp')), may hold values from -4.7683716e-06 to 4.7683716e-06
- small_m2: float32 [11, 512], P(None, ('dp', 'mp')), may hold values from 2.3060689e-14 to 1.8448551e-13
- attn_w: float32 [4, 512, 512], P(None, 'dp', 'mp'), may hold values from -0.25 to 0.25
- attn_m1: float32 [4, 512, 512], P(None, 'dp', 'mp'), may hold values from -4.7683716e-06 to 4.7683716e-06
- attn_m2: float32 [4, 512, 512], P(None, 'dp', 'mp'), may hold values from 2.3060689e-14 to 1.8448551e-13
- mlp_w: float32 [2, 512, 2048], P(None, 'dp', 'mp'), may hold values from -0.25 to 0.25
- mlp_m1: float32 [2, 512, 2048], P(None, 'dp', 'mp'), may hold values from -4.7683716e-06 to 4.7683716e-06
- mlp_m2: float32 [2, 512, 2048], P(None, 'dp', 'mp'), may hold values from 2.3060689e-14 to 1.8448551e-13
- head_w: float32 [512, 11, 256], P('dp', None, 'mp'), may hold values from -1 to 1
- head_m1: float32 [512, 11, 256], P('dp', None, 'mp'), may hold values from -4.7683716e-06 to 4.7683716e-06
- head_m2: float32 [512, 11, 256], P('dp', None, 'mp'), may hold values from 2.3060689e-14 to 1.8448551e-13
Outputs:
- loss: float32 [], replicated
- grad_norm: float32 [], replicated
- conv_new: float32 [1033, 3072], P(None, ('dp', 'mp'))
- conv_first: float32 [1033, 3072], P(None, ('dp', 'mp'))
- conv_second: float32 [1033, 3072], P(None, ('dp', 'mp'))
- cond_new: float32 [1770, 512], P(None, ('dp', 'mp'))
- cond_first: float32 [1770, 512], P(None, ('dp', 'mp'))
- cond_second: float32 [1770, 512], P(None, ('dp', 'mp'))
- small_new: float32 [11, 512], P(None, ('dp', 'mp'))
- small_first: float32 [11, 512], P(None, ('dp', 'mp'))
- small_second: float32 [11, 512], P(None, ('dp', 'mp'))
- attn_new: float32 [4, 512, 512], P(None, 'dp', 'mp')
- attn_first: float32 [4, 512, 512], P(None, 'dp', 'mp')
- attn_second: float32 [4, 512, 512], P(None, 'dp', 'mp')
- mlp_new: float32 [2, 512, 2048], P(None, 'dp', 'mp')
- mlp_first: float32 [2, 512, 2048], P(None, 'dp', 'mp')
- mlp_second: float32 [2, 512, 2048], P(None, 'dp', 'mp')
- head_new: float32 [512, 11, 256], P('dp', None, 'mp')
- head_first: float32 [512, 11, 256], P('dp', None, 'mp')
- head_second: float32 [512, 11, 256], P('dp', None, 'mp')
All inputs are finite; a program needn't handle non-finite values. No bound on the sum of `final_mask` on one device may be relied on, other than what follows from the above.
Results may differ from a plain program's by a relative error of at most 0.0091.
The roundings to bfloat16 on the way count: a program that leaves them out, or rounds other values in their place, can miss the bound.
Values may be sent and summed in bfloat16 or wider, within the bound.
A program may use at most 576 MiB of HBM per device.

v0:
```python
import functools
import math

import jax
import jax.numpy as jnp
from jax import lax
from jax.experimental import pallas as pl
from jax.experimental.pallas import tpu as pltpu
from jax.sharding import Mesh
from jax.sharding import PartitionSpec as P

f32 = jnp.float32
bf16 = jnp.bfloat16

NAMES = ("dp_0", "dp_1", "dp_2", "mp_0", "mp_1")
SIZES = {"l": 2, "z": 4, "x": 4, "h": 2, "c": 2}
RING = 4
MESH_ID = pl.DeviceIdType.MESH
ANY = pl.BlockSpec(memory_space=pl.ANY)
INVMEM = pl.BlockSpec(memory_space=pltpu.VMEM)


def here():
    low, z, x, high, core = (lax.axis_index(n) for n in NAMES)
    return {"x": x, "y": high * 2 + low, "z": z, "c": core}


def device_of(axis, at):
    if axis == "y":
        return {"dp_0": lax.rem(at, 2), "mp_0": at // 2}
    return {{"x": "dp_2", "z": "dp_1", "c": "mp_1"}[axis]: at}


def spot(dims, at):
    index = []
    for d in dims:
        if d == "l":
            index.append(lax.rem(at["y"], 2) if "y" in at else slice(None))
        elif d == "h":
            index.append(at["y"] // 2 if "y" in at else slice(None))
        else:
            index.append(at.get(d, slice(None)))
    return tuple(index)


def without(dims, axis):
    return tuple(d for d in dims if d not in ("lh" if axis == "y" else axis))


def lead(dims):
    return tuple(SIZES[d] for d in dims)


def greet(me):
    barrier = pltpu.get_barrier_semaphore()
    for axis in "xyz":
        for k in range(1, RING):
            pl.semaphore_signal(barrier, inc=1, device_id=device_of(axis, lax.rem(me[axis] + k, RING)), device_id_type=MESH_ID)
    pl.semaphore_signal(barrier, inc=1, device_id=device_of("c", 1 - me["c"]), device_id_type=MESH_ID)
    pl.semaphore_wait(barrier, 10)


def remote(src, dst, send, recv, axis, at):
    return pltpu.make_async_remote_copy(
        src_ref=src, dst_ref=dst, send_sem=send, recv_sem=recv, device_id=device_of(axis, at), device_id_type=MESH_ID
    )


def gather_kernel(plan, *refs):
    n = len(plan)
    pairs, shards = refs[0:2], refs[2 : 2 + n]
    both, outs = refs[2 + n : 4 + n], refs[4 + n : 4 + 2 * n]
    send, recv, fsend, frecv, local = refs[4 + 2 * n :]
    me = here()
    greet(me)
    swaps = []
    for i in range(2):
        mine = pltpu.make_async_copy(pairs[i], both[i].at[me["c"]], local.at[n + i])
        mine.start()
        swap = remote(pairs[i], both[i].at[me["c"]], fsend.at[n, i], frecv.at[n, i], "c", 1 - me["c"])
        swap.start()
        swaps += [mine, swap]

    def region(b, phase, pos=None):
        dims, order = plan[b]
        at = {a: me[a] for a in order[phase:]}
        if pos is not None:
            at[order[phase]] = pos
        if "c" in dims:
            at["c"] = me["c"]
        return spot(dims, at)

    def start(b, phase):
        dims, order = plan[b]
        where = outs[b].at[region(b, phase)]
        src = shards[b] if phase == 0 else where
        copies = []
        for k in (2, 1, 3):
            c = remote(src, where, send.at[b, phase, k - 1], recv.at[b, phase, k - 1], order[phase], lax.rem(me[order[phase]] + k, RING))
            c.start()
            copies.append((k, c))
        return copies

    kept = []
    for b in range(n):
        c = pltpu.make_async_copy(shards[b], outs[b].at[region(b, 0)], local.at[b])
        c.start()
        kept.append(c)
    going = [start(b, 0) for b in range(n)]
    forwards = []

    def forward(b, number, where):
        c = remote(outs[b].at[where], outs[b].at[where], fsend.at[b, number], frecv.at[b, number], "c", 1 - me["c"])
        c.start()
        forwards.append(c)

    for phase in range(3):
        for b in range(n):
            dims, order = plan[b]
            if phase == 0:
                kept[b].wait()
            nxt = None
            for k, c in going[b]:
                c.wait()
                if phase > 0 and "c" in dims:
                    forward(b, 3 * (phase - 1) + k, region(b, phase, lax.rem(me[order[phase]] + RING - k, RING)))
            if phase == 0 and "c" in dims:
                forward(b, 0, region(b, 1))
            if phase < 2:
                going[b] = start(b, phase + 1)
    for c in forwards + swaps:
        c.wait()


def gather_all(pairs, shards, plan, collective_id):
    n = len(plan)
    outs = [jax.ShapeDtypeStruct((2, *p.shape), p.dtype) for p in pairs]
    for s, (dims, _) in zip(shards, plan):
        outs.append(jax.ShapeDtypeStruct((*lead(dims), *s.shape), s.dtype))
    return pl.pallas_call(
        functools.partial(gather_kernel, plan),
        out_shape=outs,
        in_specs=[ANY] * (2 + n),
        out_specs=[ANY] * (2 + n),
        scratch_shapes=[
            pltpu.SemaphoreType.DMA((n, 3, 3)),
            pltpu.SemaphoreType.DMA((n, 3, 3)),
            pltpu.SemaphoreType.DMA((n + 1, 7)),
            pltpu.SemaphoreType.DMA((n + 1, 7)),
            pltpu.SemaphoreType.DMA((n + 2,)),
        ],
        compiler_params=pltpu.CompilerParams(collective_id=collective_id, has_side_effects=True),
    )(*pairs, *shards)


def split_index(i, sizes):
    index = []
    for s in reversed(sizes):
        index.append(lax.rem(i, s))
        i = i // s
    return tuple(reversed(index))


def add_slabs(acc, others, dims):
    sizes = lead(dims)

    def one(i, _):
        at = split_index(i, sizes)
        total = acc[at].astype(f32)
        for o in others:
            total = total + o[at].astype(f32)
        acc[at] = total.astype(acc.dtype)
        return 0

    lax.fori_loop(0, math.prod(sizes), one, 0)


def folded(v):
    total = None
    for r in range(0, v.shape[0], 8):
        for c in range(0, v.shape[1], 128):
            part = v[r : r + 8, c : c + 128]
            total = part if total is None else total + part
    return total


def scatter_kernel(plan, *refs):
    n = len(plan)
    stats, parts, stats_out, outs = refs[0], refs[1 : 1 + n], refs[1 + n], refs[2 + n : 2 + 2 * n]
    at = 2 + 2 * n
    halves, arrived = refs[at : at + n], refs[at + n : at + 2 * n]
    accs, boxes = [], []
    at += 2 * n
    for b in range(n):
        accs.append(refs[at : at + 3])
        boxes.append(refs[at + 3 : at + 6])
        at += 6
    tile, tile_box, send, recv, csend, crecv, local, tsend, trecv = refs[at:]
    me = here()
    greet(me)
    first, kept = [], []
    for b, (dims, order) in enumerate(plan):
        if "c" in dims:
            c = remote(parts[b].at[spot(dims, {"c": 1 - me["c"]})], arrived[b], csend.at[b], crecv.at[b], "c", 1 - me["c"])
            c.start()
            first.append(c)
            mine = pltpu.make_async_copy(parts[b].at[spot(dims, {"c": me["c"]})], halves[b], local.at[b])
        else:
            first.append(None)
            mine = pltpu.make_async_copy(parts[b].at[spot(dims, {order[0]: me[order[0]]})], accs[b][0], local.at[b])
        mine.start()
        kept.append(mine)

    def start(b, phase, src, dims):
        axis = plan[b][1][phase]
        copies = []
        for k in (2, 1, 3):
            pos = lax.rem(me[axis] + k, RING)
            c = remote(src.at[spot(dims, {axis: pos})], boxes[b][phase].at[k - 1], send.at[b, phase, k - 1], recv.at[b, phase, k - 1], axis, pos)
            c.start()
            copies.append(c)
        return copies

    going = [None] * n
    left = [None] * n
    ordered = [b for b in range(n) if first[b] is None] + [b for b in range(n) if first[b] is not None]
    for b in ordered:
        dims, order = plan[b]
        if first[b] is None:
            left[b] = dims
            going[b] = start(b, 0, parts[b], dims)
    for b in ordered:
        dims, order = plan[b]
        if first[b] is not None:
            left[b] = without(dims, "c")
            kept[b].wait()
            first[b].wait()
            add_slabs(halves[b], [arrived[b]], left[b])
            going[b] = start(b, 0, halves[b], left[b])
    square = jnp.zeros((8, 128), f32)
    for phase in range(3):
        for b in ordered:
            axis = plan[b][1][phase]
            rest = without(left[b], axis)
            acc, box = accs[b][phase], boxes[b][phase]
            if phase == 0 and first[b] is None:
                kept[b].wait()
            for c in going[b]:
                c.wait()
            if phase == 0:
                if first[b] is not None:
                    mine = pltpu.make_async_copy(halves[b].at[spot(left[b], {axis: me[axis]})], acc, local.at[b])
                    mine.start()
                    mine.wait()
                add_slabs(acc, [box.at[k] for k in range(3)], rest)
            elif phase == 1:
                before = accs[b][0]
                source = before.at[spot(left[b], {axis: me[axis]})]
                for i in range(math.prod(lead(rest))):
                    w = split_index(i, lead(rest))
                    total = source[w].astype(f32)
                    for k in range(3):
                        total = total + box[(k, *w)].astype(f32)
                    acc[w] = total.astype(acc.dtype)
            else:
                total = accs[b][1][spot(left[b], {axis: me[axis]})].astype(f32)
                for k in range(3):
                    total = total + box[k].astype(f32)
                outs[b][...] = total
                square = square + folded(total * total)
            left[b] = rest
            if phase < 2:
                going[b] = start(b, phase + 1, acc, rest)
    tile[0, 0:16, :] = stats[...]
    tile[0, 16:24, :] = square
    for phase, axis in enumerate("cxyz"):
        ring = 2 if axis == "c" else RING
        copies = []
        for k in range(1, ring):
            c = remote(tile.at[phase], tile_box.at[phase, k - 1], tsend.at[phase, k - 1], trecv.at[phase, k - 1], axis, lax.rem(me[axis] + k, ring))
            c.start()
            copies.append(c)
        total = tile[phase]
        for k, c in enumerate(copies):
            c.wait()
        for k, c in enumerate(copies):
            total = total + tile_box[phase, k]
        tile[phase + 1] = total
    stats_out[...] = tile[4]


def scatter_all(stats, parts, plan, collective_id):
    n = len(plan)
    outs = [jax.ShapeDtypeStruct((24, 128), f32)]
    halves, arrived, later = [], [], []
    for p, (dims, order) in zip(parts, plan):
        slab = p.shape[-2:]
        outs.append(jax.ShapeDtypeStruct(slab, f32))
        rest = dims
        if "c" in dims:
            rest = without(dims, "c")
            halves.append(pltpu.VMEM((*lead(rest), *slab), p.dtype))
            arrived.append(pltpu.VMEM((*lead(rest), *slab), p.dtype))
        else:
            halves.append(pltpu.VMEM((8, 128), p.dtype))
            arrived.append(pltpu.VMEM((8, 128), p.dtype))
        accs, boxes = [], []
        for axis in order:
            rest = without(rest, axis)
            accs.append(pltpu.VMEM((*lead(rest), *slab), p.dtype))
            boxes.append(pltpu.VMEM((3, *lead(rest), *slab), p.dtype))
        later += accs + boxes
    return pl.pallas_call(
        functools.partial(scatter_kernel, plan),
        out_shape=outs,
        in_specs=[INVMEM] + [ANY] * n,
        out_specs=[INVMEM] * (1 + n),
        scratch_shapes=[
            *halves,
            *arrived,
            *later,
            pltpu.VMEM((5, 24, 128), f32),
            pltpu.VMEM((4, 3, 24, 128), f32),
            pltpu.SemaphoreType.DMA((n, 3, 3)),
            pltpu.SemaphoreType.DMA((n, 3, 3)),
            pltpu.SemaphoreType.DMA((n,)),
            pltpu.SemaphoreType.DMA((n,)),
            pltpu.SemaphoreType.DMA((n,)),
            pltpu.SemaphoreType.DMA((4, 3)),
            pltpu.SemaphoreType.DMA((4, 3)),
        ],
        compiler_params=pltpu.CompilerParams(collective_id=collective_id, has_side_effects=True, vmem_limit_bytes=56 * 2**20),
    )(stats, *parts)


OWNED = ("l", "z", "x", "h")
GATHER = (
    (OWNED, ("x", "z", "y")),
    (OWNED, ("x", "z", "y")),
    (OWNED, ("x", "z", "y")),
    (("c", *OWNED), ("z", "y", "x")),
    (("h", "c", "l", "z", "x"), ("y", "x", "z")),
    (("h", "c", "l", "z", "x"), ("z", "y", "x")),
)
SCATTER = (
    (OWNED, ("x", "z", "y")),
    (OWNED, ("x", "z", "y")),
    (OWNED, ("x", "z", "y")),
    (OWNED, ("z", "y", "x")),
    (("h", "l", "z", "x"), ("y", "x", "z")),
    (("h", "l", "z", "x"), ("z", "y", "x")),
)

D, EXP, MAP, PIX = 512, 3072, 9, 81
PAIR = 24
WIDTH = 384
OWNERS = WIDTH // 24
CHUNK = 3
SPAN = CHUNK * MAP * PAIR
EXPAND = 8.0 / math.sqrt(D)
PROJECT = 8.0 / math.sqrt(EXP)
VMEM_BYTES = 60 * 2**20


def sigmoid(v):
    return 0.5 + 0.5 * jnp.tanh(0.5 * v)


def nt(left, right):
    return lax.dot_general(left, right, (((1,), (1,)), ((), ())), preferred_element_type=f32)


def nn(left, right):
    return lax.dot_general(left, right, (((1,), (0,)), ((), ())), preferred_element_type=f32)


def tn(left, right):
    return lax.dot_general(left, right, (((0,), (0,)), ((), ())), preferred_element_type=f32)


def clear_borders(padded):
    zero = jnp.zeros((MAP, PAIR, WIDTH), f32)
    padded[0] = zero
    padded[MAP + 1] = zero


def each_block(body):
    def one(row, _):
        for lane in range(WIDTH // 128):
            for group in range(PAIR // 8):
                body(row, slice(8 * group, 8 * group + 8), slice(128 * lane, 128 * lane + 128))
        return 0

    lax.fori_loop(0, MAP, one, 0)


def forward_kernel(frames, expand, project, taps, pre, deep, out, act):
    step = pl.program_id(0)

    @pl.when(step == 0)
    def _():
        clear_borders(act)
        out[...] = jnp.zeros_like(out)

    weight = expand[...].reshape(WIDTH, D)
    back = project[...].reshape(WIDTH, D)

    def enter(i, _):
        rows = pl.ds(pl.multiple_of(i * SPAN, SPAN), SPAN)
        e = nt(frames[rows, :], weight) * EXPAND
        e = e.reshape(CHUNK * MAP, PAIR, WIDTH)
        pre[pl.ds(i * CHUNK * MAP, CHUNK * MAP)] = e
        act[pl.ds(1 + i * CHUNK, CHUNK)] = (e * sigmoid(e)).reshape(CHUNK, MAP, PAIR, WIDTH)
        return 0

    lax.fori_loop(0, MAP // CHUNK, enter, 0)

    def mix(row, subs, lanes):
        near = act[pl.ds(row, 3), :, subs, lanes]
        tap = [jnp.broadcast_to(taps[t : t + 1, lanes], (8, 128)) for t in range(9)]
        for col in range(MAP):
            total = None
            for t in range(9):
                at = col + t % 3 - 1
                if 0 <= at < MAP:
                    term = near[t // 3, at] * tap[t]
                    total = term if total is None else total + term
            deep[row * MAP + col, subs, lanes] = total

    each_block(mix)

    def leave(i, _):
        rows = pl.ds(pl.multiple_of(i * SPAN, SPAN), SPAN)
        v = deep[pl.ds(i * CHUNK * MAP, CHUNK * MAP)].reshape(SPAN, WIDTH)
        out[rows, :] += nn((v * sigmoid(v)).astype(bf16), back) * PROJECT
        return 0

    lax.fori_loop(0, MAP // CHUNK, leave, 0)


def conv_forward(frames, expand, project, taps):
    steps = expand.shape[0] // OWNERS
    channels = steps * WIDTH
    whole = pl.BlockSpec((PIX * PAIR, D), lambda i: (0, 0))
    weights = pl.BlockSpec((OWNERS, 24, D), lambda i: (i, 0, 0))
    maps = pl.BlockSpec((PIX, PAIR, WIDTH), lambda i: (0, 0, i))
    small = pl.BlockSpec((9, WIDTH), lambda i: (0, i))
    kept = jax.ShapeDtypeStruct((PIX, PAIR, channels), f32)
    return pl.pallas_call(
        forward_kernel,
        grid=(steps,),
        out_shape=[kept, kept, jax.ShapeDtypeStruct((PIX * PAIR, D), f32)],
        in_specs=[whole, weights, weights, small],
        out_specs=[maps, maps, whole],
        scratch_shapes=[pltpu.VMEM((MAP + 2, MAP, PAIR, WIDTH), f32)],
        compiler_params=pltpu.CompilerParams(vmem_limit_bytes=VMEM_BYTES),
    )(frames, expand, project, taps)


def backward_kernel(frames, grads, project, taps, pre, deep, dexpand, dproject, dtaps, spread, mid, dpre, acc):
    step = pl.program_id(0)

    @pl.when(step == 0)
    def _():
        clear_borders(spread)

    back = project[...].reshape(WIDTH, D)

    def enter(i, _):
        rows = pl.ds(pl.multiple_of(i * SPAN, SPAN), SPAN)
        dmid = nt(grads[rows, :], back) * PROJECT
        v = deep[pl.ds(i * CHUNK * MAP, CHUNK * MAP)].reshape(SPAN, WIDTH)
        s = sigmoid(v)
        m = v * s
        mid[rows, :] = m.astype(bf16)
        dv = dmid * (s + m * (1.0 - s))
        spread[pl.ds(1 + i * CHUNK, CHUNK)] = dv.reshape(CHUNK, MAP, PAIR, WIDTH)
        return 0

    lax.fori_loop(0, MAP // CHUNK, enter, 0)
    acc[...] = jnp.zeros_like(acc)

    def mix(row, subs, lanes):
        near = spread[pl.ds(row, 3), :, subs, lanes]
        tap = [jnp.broadcast_to(taps[t : t + 1, lanes], (8, 128)) for t in range(9)]
        sums = [None] * 9
        for col in range(MAP):
            e = pre[row * MAP + col, subs, lanes]
            s = sigmoid(e)
            a = e * s
            total = None
            for t in range(9):
                at = col + 1 - t % 3
                if 0 <= at < MAP:
                    g = near[2 - t // 3, at]
                    term = g * tap[t]
                    total = term if total is None else total + term
                    term = g * a
                    sums[t] = term if sums[t] is None else sums[t] + term
            dpre[row * MAP + col, subs, lanes] = total * (s + a * (1.0 - s))
        for t in range(9):
            acc[t, :, lanes] += sums[t]

    each_block(mix)
    dtaps[...] = jnp.sum(acc[...], axis=1) * (8.0 / 3.0)
    low = dpre[...].reshape(PIX * PAIR, WIDTH).astype(bf16)
    dexpand[...] = (tn(low, frames[...]) * EXPAND).astype(bf16).reshape(OWNERS, 24, D)
    dproject[...] = (tn(mid[...], grads[...]) * PROJECT).astype(bf16).reshape(OWNERS, 24, D)


def conv_backward(frames, grads, project, taps, pre, deep):
    steps = project.shape[0] // OWNERS
    channels = steps * WIDTH
    whole = pl.BlockSpec((PIX * PAIR, D), lambda i: (0, 0))
    weights = pl.BlockSpec((OWNERS, 24, D), lambda i: (i, 0, 0))
    maps = pl.BlockSpec((PIX, PAIR, WIDTH), lambda i: (0, 0, i))
    small = pl.BlockSpec((9, WIDTH), lambda i: (0, i))
    owned = jax.ShapeDtypeStruct((OWNERS * steps, 24, D), bf16)
    return pl.pallas_call(
        backward_kernel,
        grid=(steps,),
        out_shape=[owned, owned, jax.ShapeDtypeStruct((9, channels), f32)],
        in_specs=[whole, whole, weights, small, maps, maps],
        out_specs=[weights, weights, small],
        scratch_shapes=[
            pltpu.VMEM((MAP + 2, MAP, PAIR, WIDTH), f32),
            pltpu.VMEM((PIX * PAIR, WIDTH), bf16),
            pltpu.VMEM((PIX, PAIR, WIDTH), f32),
            pltpu.VMEM((9, 8, WIDTH), f32),
        ],
        compiler_params=pltpu.CompilerParams(vmem_limit_bytes=VMEM_BYTES),
    )(frames, grads, project, taps, pre, deep)

INSTR, DIMS, BINS, NTOK, FRAMES, HEADS, HD = 744, 11, 256, 8, 6, 8, 64
TABLE = INSTR + 2
ROWS = PAIR * NTOK
SMALL_AT = TABLE - D
LN_EPS = 1e-06
OUT_MULT = 2.0
HIGH = lax.Precision.HIGHEST
FILM = 16.0 / math.sqrt(D)
LEARN = 4.0 / math.sqrt(D)


def norm_fwd(x, gain):
    centre = x - jnp.mean(x, -1, keepdims=True)
    inverse = lax.rsqrt(jnp.mean(centre * centre, -1, keepdims=True) + LN_EPS)
    normed = centre * inverse
    return normed * (1.0 + gain), normed, inverse


def norm_back(normed, inverse, gain, grad_out):
    dnormed = grad_out * (1.0 + gain)
    grad_in = inverse * (
        dnormed
        - jnp.mean(dnormed, -1, keepdims=True)
        - normed * jnp.mean(dnormed * normed, -1, keepdims=True)
    )
    return grad_in, jnp.sum(grad_out * normed, 0, keepdims=True)


def gelu_parts(u):
    c = math.sqrt(2.0 / math.pi)
    square = u * u
    t = jnp.tanh(c * u * (1.0 + 0.044715 * square))
    half = 0.5 * (1.0 + t)
    return u * half, half + 0.5 * u * (1.0 - t * t) * c * (1.0 + 3.0 * 0.044715 * square)


def iota(shape, axis):
    return lax.broadcasted_iota(jnp.int32, shape, axis)


def shifted(v, places):
    tiles = [pltpu.roll(v[:, i : i + 128], (128 - places) % 128, 1) for i in range(0, v.shape[1], 128)]
    return jnp.concatenate(tiles, axis=1)


def only(v, first):
    place = iota(v.shape, 1) & 15
    return jnp.where((place >= first) & (place < first + 4), v, 0.0)


def place_of_feature(start, rows):
    d = iota((rows, D), 1)
    owner = d >> 2
    row = (owner & 1) * 1024 + (owner >> 1) * 16 + 12 + (d & 3)
    return (iota((rows, D), 0) + start == row).astype(bf16)


def middle_kernel(
    core_ref, own, other, cells, misc, one, two, instr, cam, bins, mask,
    dcells, dmisc, done_one, done_two, stats,
    y, logit, att, qkv, prob, ctx, up, hid, acc, dlog, lowgrad,
):
    core = core_ref[0]
    lanes = iota((PAIR, 128), 1)

    def chosen(tile):
        at = lanes + 128 * tile
        return ((at == instr[...]) | (at == INSTR + cam[0] + cam[1])).astype(f32)

    choose_lo = jnp.concatenate([chosen(i) for i in range(4)], axis=1).astype(bf16)
    choose_hi = jnp.concatenate([chosen(i) for i in range(4, 8)], axis=1).astype(bf16)
    flat = misc[...]
    cvec = only(shifted(nt(choose_lo, flat), 8) + shifted(nt(choose_hi, flat), 12), 0).astype(bf16).astype(f32)
    cvec_4 = shifted(cvec, 124)
    cvec_low, cvec_4_low = cvec.astype(bf16), cvec_4.astype(bf16)
    gamma = nn(cvec_low, flat) * FILM
    beta = nn(cvec_4_low, flat) * FILM
    scale = 1.0 + gamma
    pick = (iota((16, D), 1) == SMALL_AT + iota((16, D), 0)).astype(bf16)
    small = nn(nt(pick, flat).astype(bf16), place_of_feature(0, 2048))
    gains = [small[i : i + 1] for i in range(3)]
    learner = jnp.concatenate([small[3:11], jnp.zeros((120, D), f32)], axis=0)

    def feature(cell, _):
        rows = pl.ds(pl.multiple_of(cell * PAIR, PAIR), PAIR)
        v = cells[rows, :].astype(f32) + (own[rows, :] + other[rows, :]) * scale + beta
        y[rows, :] = v
        return 0

    lax.fori_loop(0, PIX, feature, 0)
    logit[...] = (
        lax.dot_general(y[...], learner, (((1,), (1,)), ((), ())), precision=HIGH, preferred_element_type=f32) * LEARN
    )

    def softmax_over_cells(v):
        v = v.reshape(PIX, PAIR, 128)
        e = jnp.exp(v - jnp.max(v, 0, keepdims=True))
        return e / jnp.sum(e, 0, keepdims=True)

    att[...] = softmax_over_cells(logit[...]).reshape(PIX * PAIR, 128)
    acc[...] = jnp.zeros_like(acc)
    for half in range(2):
        columns = slice(256 * half, 256 * half + 256)

        zero = jnp.zeros((PAIR, 256), f32)
        for t0 in range(0, NTOK, 4):

            def gather_some(cell, totals, t0=t0, columns=columns):
                rows = pl.ds(pl.multiple_of(cell * PAIR, PAIR), PAIR)
                a, v = att[rows, :], y[rows, columns]
                return tuple(t + a[:, t0 + i : t0 + i + 1] * v for i, t in enumerate(totals))

            totals = lax.fori_loop(0, PIX, gather_some, (zero,) * 4)
            for i in range(4):
                acc[(t0 + i) * PAIR : (t0 + i + 1) * PAIR, columns] = totals[i]
    tok = acc[...].astype(bf16).astype(f32)

    h1, normed1, inverse1 = norm_fwd(tok, gains[0])
    h1_low = h1.astype(bf16)
    row_q, row_k = iota((ROWS, ROWS), 0), iota((ROWS, ROWS), 1)
    image_q, image_k = lax.rem(row_q, PAIR), lax.rem(row_k, PAIR)
    order_q = image_q * NTOK + lax.div(row_q, PAIR)
    order_k = image_k * NTOK + lax.div(row_k, PAIR)
    seen = (lax.div(image_q, FRAMES) == lax.div(image_k, FRAMES)) & (order_k <= order_q)
    root = HD**-0.5
    acc[...] = jnp.zeros_like(acc)

    def attend(m, _):
        p = nn(h1_low, one[m, :, 0:384]).astype(bf16)
        qkv[m] = p
        outs = []
        for head in range(2):
            q, k, v = (p[:, 128 * j + 64 * head : 128 * j + 64 * head + 64] for j in range(3))
            s = jnp.where(seen, nt(q, k) * root, -1e30)
            e = jnp.exp(s - jnp.max(s, -1, keepdims=True))
            w = e / jnp.sum(e, -1, keepdims=True)
            prob[m, head] = w
            outs.append(nn(w.astype(bf16), v))
        o = jnp.concatenate(outs, axis=1).astype(bf16)
        ctx[m] = o
        acc[...] += nt(o, one[m, :, 384:512])
        return 0

    lax.fori_loop(0, 4, attend, 0)
    x1 = tok + OUT_MULT * acc[...]
    h2, normed2, inverse2 = norm_fwd(x1, gains[1])
    h2_low = h2.astype(bf16)
    acc[...] = x1

    def feed(m, _):
        u = nn(h2_low, two[m, :, 0:512])
        up[m] = u
        low = gelu_parts(u)[0].astype(bf16)
        hid[m] = low
        acc[...] += nt(low, two[m, :, 512:1024])
        return 0

    lax.fori_loop(0, 4, feed, 0)
    x2 = acc[...]
    normed_out, normed3, inverse3 = norm_fwd(x2, gains[2])
    pooled = (jnp.sum(normed_out.reshape(NTOK, PAIR, D), axis=0) * (1.0 / NTOK)).astype(bf16)

    low_half = lanes < 64
    scores = [nn(pooled, one[m, :, 512:1280]) for m in range(4)]
    weight = mask[...]
    loss = jnp.zeros((PAIR, 128), f32)
    for u in range(6):
        tiles = [s[:, 128 * u : 128 * u + 128] for s in scores]
        top = jnp.maximum(jnp.maximum(tiles[0], tiles[1]), jnp.maximum(tiles[2], tiles[3]))
        left = jnp.max(jnp.where(low_half, top, -jnp.inf), -1, keepdims=True)
        right = jnp.max(jnp.where(low_half, -jnp.inf, top), -1, keepdims=True)
        top = jnp.where(low_half, left, right)
        total = sum(jnp.exp(t - top) for t in tiles)
        left = jnp.sum(jnp.where(low_half, total, 0.0), -1, keepdims=True)
        right = jnp.sum(jnp.where(low_half, 0.0, total), -1, keepdims=True)
        lse = top + jnp.log(jnp.where(low_half, left, right))
        label = jnp.where(low_half, bins[:, 2 * u : 2 * u + 1], bins[:, 2 * u + 1 : 2 * u + 2])
        real = low_half | (2 * u + 1 < DIMS)
        target = jnp.zeros((PAIR, 128), f32)
        for m, t in enumerate(tiles):
            hit = label == (lanes & 63) + 64 * m
            target = target + jnp.where(hit, t, 0.0)
            slope = weight * (jnp.exp(t - lse) - hit.astype(f32))
            dlog[m, :, 128 * u : 128 * u + 128] = jnp.where(real, slope, 0.0).astype(bf16)
        counted = real & ((lanes & 63) == 0)
        loss = loss + weight * (jnp.where(counted, lse, 0.0) - target)
    stats[...] = jnp.zeros_like(stats)
    stats[0:8] = loss[0:8] + loss[8:16] + loss[16:24]
    counts = jnp.where(lanes == 0, weight, 0.0)
    stats[8:16] = counts[0:8] + counts[8:16] + counts[16:24]
    dpooled = jnp.zeros((PAIR, D), f32)
    for m in range(4):
        dpooled = dpooled + nt(dlog[m], one[m, :, 512:1280])
    dnormed = jnp.broadcast_to(dpooled * (1.0 / NTOK), (NTOK, PAIR, D)).reshape(ROWS, D)
    dx2, dgain2 = norm_back(normed3, inverse3, gains[2], dnormed)
    dbranch = dx2.astype(bf16)
    acc[...] = jnp.zeros_like(acc)

    def feed_back(m, _):
        slope = gelu_parts(up[m])[1]
        dup = (nn(dbranch, two[m, :, 512:1024]) * slope).astype(bf16)
        lowgrad[m] = dup
        acc[...] += nt(dup, two[m, :, 0:512])
        return 0

    lax.fori_loop(0, 4, feed_back, 0)
    dx1_norm, dgain1 = norm_back(normed2, inverse2, gains[1], acc[...])
    dx1 = dx2 + dx1_norm
    dattn = dx1.astype(bf16)

    def feed_weights(h, _):
        m = 2 * h + core
        done_one[h, :, 512:1280] = tn(pooled, dlog[m]).astype(bf16)
        done_two[h, :, 0:512] = tn(h2_low, lowgrad[m]).astype(bf16)
        done_two[h, :, 512:1024] = tn(dbranch, hid[m]).astype(bf16)
        done_one[h, :, 384:512] = (tn(dattn, ctx[m]) * OUT_MULT).astype(bf16)
        return 0

    lax.fori_loop(0, 2, feed_weights, 0)
    acc[...] = jnp.zeros_like(acc)

    def attend_back(m, _):
        do = (nn(dattn, one[m, :, 384:512]) * OUT_MULT).astype(bf16)
        p = qkv[m]
        dq, dk, dv = [], [], []
        for head in range(2):
            q, k, v = (p[:, 128 * j + 64 * head : 128 * j + 64 * head + 64] for j in range(3))
            w = prob[m, head]
            d = do[:, 64 * head : 64 * head + 64]
            dp = nt(d, v)
            dv.append(tn(w.astype(bf16), d))
            ds = (w * (dp - jnp.sum(w * dp, -1, keepdims=True))).astype(bf16)
            dq.append(nn(ds, k) * root)
            dk.append(tn(ds, q) * root)
        g = jnp.concatenate([*dq, *dk, *dv], axis=1).astype(bf16)
        lowgrad[m, :, 0:384] = g
        acc[...] += nt(g, one[m, :, 0:384])
        return 0

    lax.fori_loop(0, 4, attend_back, 0)

    def attend_weights(h, _):
        done_one[h, :, 0:384] = tn(h1_low, lowgrad[2 * h + core, :, 0:384]).astype(bf16)
        return 0

    lax.fori_loop(0, 2, attend_weights, 0)
    dtok_norm, dgain0 = norm_back(normed1, inverse1, gains[0], acc[...])
    acc[...] = dx1 + dtok_norm

    def slope_of(cell, _):
        rows = pl.ds(pl.multiple_of(cell * PAIR, PAIR), PAIR)
        v = y[rows, :]
        found = jnp.zeros((PAIR, 128), f32)
        for t in range(NTOK):
            s = jnp.sum(v * acc[t * PAIR : (t + 1) * PAIR, :], -1, keepdims=True)
            found = jnp.where(lanes == t, s, found)
        logit[rows, :] = found
        return 0

    lax.fori_loop(0, PIX, slope_of, 0)
    a = att[...].reshape(PIX, PAIR, 128)
    da = logit[...].reshape(PIX, PAIR, 128)
    logit[...] = (a * (da - jnp.sum(a * da, 0, keepdims=True)) * LEARN).reshape(PIX * PAIR, 128)
    dlearner = lax.dot_general(logit[...], y[...], (((0,), (0,)), ((), ())), precision=HIGH, preferred_element_type=f32)

    def spread(cell, sums):
        rows = pl.ds(pl.multiple_of(cell * PAIR, PAIR), PAIR)
        a, dl = att[rows, :], logit[rows, :]
        dy = jnp.zeros((PAIR, D), f32)
        for t in range(NTOK):
            dy = dy + a[:, t : t + 1] * acc[t * PAIR : (t + 1) * PAIR, :] + dl[:, t : t + 1] * learner[t : t + 1]
        dcells[rows, :] = (dy * scale).astype(bf16)
        return sums[0] + dy * (own[rows, :] + other[rows, :]), sums[1] + dy

    zero = jnp.zeros((PAIR, D), f32)
    dgamma, dbeta = lax.fori_loop(0, PIX, spread, (zero, zero))
    dgamma, dbeta = dgamma.astype(bf16), dbeta.astype(bf16)
    dcvec = only(nt(dgamma, flat) + shifted(nt(dbeta, flat), 4), 0) * FILM
    high = dcvec.astype(bf16).astype(f32)
    rest = dcvec - high
    dsmall = jnp.concatenate([dgain0, dgain1, dgain2, dlearner[0:8], jnp.zeros((5, D), f32)], axis=0).astype(bf16)
    mine = pl.ds(pl.multiple_of(core * 1024, 1024), 1024)
    lhs = jnp.concatenate(
        [cvec, cvec_4, shifted(high, 120), shifted(rest, 120), shifted(high, 116), shifted(rest, 116)], axis=0
    )
    lhs = jnp.where(core == 0, lhs[:, 0:1024], lhs[:, 1024:2048])
    lhs = jnp.concatenate([lhs, nt(dsmall, place_of_feature(core * 1024, 1024))], axis=0).astype(bf16)
    rhs = jnp.concatenate([dgamma, dbeta, choose_lo, choose_lo, choose_hi, choose_hi, pick], axis=0)
    result = tn(lhs, rhs)
    film_rows = (iota((1024, D), 0) & 15) < 8
    dmisc[...] = jnp.where(film_rows, result * FILM, result).astype(bf16)


def middle(core, own, other, cells, misc, one, two, instr, cam, bins, mask):
    vmem = pl.BlockSpec(memory_space=pltpu.VMEM)
    return pl.pallas_call(
        middle_kernel,
        out_shape=[
            jax.ShapeDtypeStruct((PIX * PAIR, D), bf16),
            jax.ShapeDtypeStruct((1024, D), bf16),
            jax.ShapeDtypeStruct((2, D, 1280), bf16),
            jax.ShapeDtypeStruct((2, D, 1024), bf16),
            jax.ShapeDtypeStruct((16, 128), f32),
        ],
        in_specs=[pl.BlockSpec(memory_space=pltpu.SMEM)] + [vmem] * 10,
        out_specs=[vmem] * 5,
        scratch_shapes=[
            pltpu.VMEM((PIX * PAIR, D), f32),
            pltpu.VMEM((PIX * PAIR, 128), f32),
            pltpu.VMEM((PIX * PAIR, 128), f32),
            pltpu.VMEM((4, ROWS, 384), bf16),
            pltpu.VMEM((4, 2, ROWS, ROWS), f32),
            pltpu.VMEM((4, ROWS, 128), bf16),
            pltpu.VMEM((4, ROWS, 512), f32),
            pltpu.VMEM((4, ROWS, 512), bf16),
            pltpu.VMEM((ROWS, D), f32),
            pltpu.VMEM((4, PAIR, 768), bf16),
            pltpu.VMEM((4, ROWS, 512), bf16),
        ],
        compiler_params=pltpu.CompilerParams(vmem_limit_bytes=VMEM_BYTES),
    )(core, own, other, cells, misc, one, two, instr, cam, bins, mask)

TAIL = TABLE + 11
IMAGES = 12
MP = ("mp_0", "mp_1")
DP_MP = NAMES
DP = ("dp_0", "dp_1", "dp_2")
CLIP_NORM = 0.02
BETA_ONE = 0.9
BETA_TWO = 0.999
ADAM_EPS = 1e-08
DECAY = 0.01
RATES = (0.1, 0.1, 0.2, 0.05, 0.05, 0.2)


def adam(master, first, second, grad, t, rate):
    first_new = BETA_ONE * first + (1.0 - BETA_ONE) * grad
    second_new = BETA_TWO * second + (1.0 - BETA_TWO) * grad * grad
    m_hat = first_new / (1.0 - BETA_ONE**t)
    v_hat = second_new / (1.0 - BETA_TWO**t)
    master_new = master - rate * (m_hat / (jnp.sqrt(v_hat) + ADAM_EPS) + DECAY * master)
    return [master_new, first_new, second_new]


def pack_misc(film, table, small):
    tail = jnp.concatenate([table, small], axis=1)
    tail = jnp.pad(tail, ((0, 0), (0, 2 * D - tail.shape[1])))
    return jnp.concatenate([film[:, :D], film[:, D:], tail[:, :D], tail[:, D:]], axis=0)


def unpack_misc(misc):
    film = jnp.concatenate([misc[0:4], misc[4:8]], axis=1)
    tail = jnp.concatenate([misc[8:12], misc[12:16]], axis=1)
    return film, tail[:, :TABLE], tail[:, TABLE:TAIL]


def pack_attn_head(attn, head):
    both = jnp.concatenate([*attn, head], axis=-1)
    return jnp.pad(both, [(0, 0)] * (both.ndim - 1) + [(0, 1280 - both.shape[-1])])


def swap_cores(value):
    return lax.ppermute(value, "mp_1", [(0, 1), (1, 0)])


def per_device(
    frames, camera_ids, instruction_ids, action_bins, final_mask, step_count,
    conv_w, conv_m1, conv_m2, cond_w, cond_m1, cond_m2, small_w, small_m1, small_m2,
    attn_w, attn_m1, attn_m2, mlp_w, mlp_m1, mlp_m2, head_w, head_m1, head_m2,
):
    core, high = lax.axis_index("mp_1"), lax.axis_index("mp_0")
    conv_t = conv_w.T.astype(bf16)
    cond_t = cond_w.T.astype(bf16)
    attn_l = attn_w.astype(bf16)
    shards = (
        conv_t[:, :D],
        conv_t[:, D : 2 * D],
        jnp.pad(conv_w[2 * D :].astype(bf16), ((0, 7), (0, 104))),
        pack_misc(cond_t[:, : 2 * D], cond_t[:, 2 * D :], small_w.T.astype(bf16)),
        pack_attn_head([attn_l[j] for j in range(4)], head_w.astype(bf16).reshape(16, DIMS * 64)),
        jnp.moveaxis(mlp_w.astype(bf16), 0, 1).reshape(16, 1024),
    )
    image = jnp.arange(PAIR)
    cam = jnp.where(image // IMAGES == core, jnp.tile(camera_ids, 2), 0)
    cam = jnp.broadcast_to(cam[:, None], (PAIR, 128))
    frames2, cam2, expand, project, taps_all, misc_all, one_all, two_all = gather_all(
        (frames, cam), shards, GATHER, 1
    )
    expand = expand.reshape(64, 24, D)
    project = project.reshape(64, 24, D)
    taps = taps_all.reshape(64, 16, 128)[:, :9, :24].astype(f32) * (8.0 / 3.0)
    taps = taps.transpose(1, 0, 2).reshape(9, 1536)

    cells = frames2.transpose(2, 0, 1, 3).reshape(PIX * PAIR, D)
    pre, deep, part = conv_forward(cells, expand, project, taps)
    other = swap_cores(part)
    instr = jnp.repeat(lax.dynamic_slice_in_dim(instruction_ids, high * 4, 4), FRAMES)
    bins = jnp.pad(
        lax.dynamic_slice_in_dim(action_bins, high * PAIR, PAIR), ((0, 0), (0, 128 - DIMS)), constant_values=-1
    )
    mask = lax.dynamic_slice_in_dim(final_mask, high * PAIR, PAIR).astype(f32)
    dcells, dmisc, done_one, done_two, stats = middle(
        core[None],
        part,
        other,
        cells,
        misc_all.reshape(2048, D),
        one_all.reshape(4, D, 1280),
        two_all.reshape(4, D, 1024),
        jnp.broadcast_to(instr[:, None], (PAIR, 128)),
        cam2,
        bins,
        jnp.broadcast_to(mask[:, None], (PAIR, 128)),
    )
    dexpand, dproject, dtaps = conv_backward(cells, dcells, project, taps, pre, deep)
    dtaps = dtaps.astype(bf16).reshape(9, 64, 24).transpose(1, 0, 2)
    dtaps = jnp.pad(dtaps, ((0, 0), (0, 7), (0, 104)))
    parts = [
        g.reshape(*lead(dims), *s.shape)
        for g, s, (dims, _) in zip((dexpand, dproject, dtaps, dmisc, done_one, done_two), shards, SCATTER)
    ]
    totals, gexpand, gproject, gtaps, gmisc, gone, gtwo = scatter_all(stats, parts, SCATTER, 2)
    gfilm, gtable, gsmall = unpack_misc(gmisc)
    grads = (
        jnp.concatenate([gexpand.T, gproject.T, gtaps[:9, :24]], 0),
        jnp.concatenate([gfilm, gtable], 1).T,
        gsmall.T,
        jnp.stack([gone[:, 128 * j : 128 * j + 128] for j in range(4)]),
        jnp.moveaxis(gtwo.reshape(16, 2, 512), 1, 0),
        gone[:, 512 : 512 + DIMS * 64].reshape(16, DIMS, 64),
    )
    loss_sum, count, square = (jnp.sum(totals[8 * i : 8 * i + 8]) for i in range(3))
    loss_sum, count = 0.5 * loss_sum, 0.5 * count
    norm = jnp.sqrt(square) / count
    factor = jnp.minimum(1.0, CLIP_NORM / norm) / count
    steps_done = step_count[0].astype(f32)
    masters = (conv_w, cond_w, small_w, attn_w, mlp_w, head_w)
    firsts = (conv_m1, cond_m1, small_m1, attn_m1, mlp_m1, head_m1)
    seconds = (conv_m2, cond_m2, small_m2, attn_m2, mlp_m2, head_m2)
    outs = [loss_sum / count, norm]
    for idx in range(6):
        outs.extend(adam(masters[idx], firsts[idx], seconds[idx], grads[idx] * factor, steps_done, RATES[idx]))
    return tuple(outs)


def solution(mesh):
    torus = Mesh(mesh.devices.reshape(2, 4, 4, 2, 2), NAMES)
    weights = (
        *[P(None, DP_MP)] * 9,
        *[P(None, DP, MP)] * 6,
        *[P(DP, None, MP)] * 3,
    )
    data = (P(DP_MP, None, None), P(DP_MP), P(DP), P(DP, None), P(DP), P())
    return jax.shard_map(
        per_device, mesh=torus, in_specs=(*data, *weights), out_specs=(P(), P(), *weights), check_vma=False
    )
```

profile of v0, /device:TPU:1, one launch (start us, length us, event | category | flops | bytes accessed | tf_op | source)
XLA Modules:
  0.0 366.4 jit_solution(12828983518928777684)
XLA Ops:
  0.7 0.0 copy-start
  0.7 0.8 convert_bitcast_fusion.1
  1.4 0.7 convert_bitcast_fusion.2
  2.1 0.8 convert_element_type.55
  2.9 0.9 convert_element_type.56
  3.8 0.1 reshape.128
  4.0 1.1 copy.58
  5.1 0.7 copy.61.refs_2_
  5.8 0.7 copy.62.refs_3_
  6.5 0.7 tile.4
  7.1 0.1 tile.10
  7.2 0.6 pad.22.refs_6_
  7.9 0.6 pad.20.refs_4_
  8.5 0.8 convert_bitcast_fusion
  9.3 0.6 copy.80
  9.9 0.1 fusion.29
  10.0 0.6 pad_maximum_fusion.1.refs_5_
  10.6 0.7 broadcast_in_dim.28.refs_1_
  11.3 99.7 %shard_map.383 = (bf16[2,12,81,512]{3,2,1,0:T(8,128)(2,1)}, s32[2,24,128]{2,1,0:T(8,128)}, bf16[2,4,4,2,24,512]{5,4,3,2,1,0:T(8,128)(2,1)}, bf16[2,4,4,2,24,512]...) custom-call(bf16[12,81,512]{2,1,0:T(8,128)(2,1)} %refs_0_.1, ...), custom_call_target="tpu_custom_call" | custom-call | tf_op jit(solution)/shard_map/pallas_call | solution.py:140
  111.0 2.4 copy.63
  113.4 2.0 reshape.130.frames.cells
  115.5 0.8 reshape.134.taps
  116.3 26.2 %shard_map.384 = (f32[81,24,1536]{2,1,0:T(8,128)}, f32[81,24,1536]{2,1,0:T(8,128)}, f32[1944,512]{1,0:T(8,128)}) custom-call(bf16[1944,512]{1,0:T(8,128)(2,1)} %reshape.130.frames.cells, bf16[64,24,512]{2,1,0:T(8,128)(2,1)} %bitcast.100, bf16[64,24,512]{2,1,0:T(8,128)(2,1)} %bitcast.92, f32[9,1536]{1,0:T(8,128)} %reshape.134.taps), custom_call_target="tpu_custom_call" | custom-call | tf_op jit(solution)/shard_map/pallas_call | solution.py:449
  142.5 0.2 collective-permute-start
  142.7 0.1 constant_dynamic-slice_fusion
  142.8 0.1 copy.77
  142.9 0.1 dynamic_slice.9
  142.9 0.1 broadcast_in_dim.29
  143.0 0.1 broadcast_in_dim.30
  143.8 0.6 pad.23.bins
  144.4 0.1 dynamic-slice_convert_fusion
  144.5 5.3 %collective-permute-done.other = f32[1944,512]{1,0:T(8,128)} collective-permute-done((f32[1944,512]{1,0:T(8,128)}, f32[1944,512]{1,0:T(8,128)}, u32[]{:S(2)}, u32[]{:S(2)}) %collective-permute-start) | collective-permute-done | bytes 3981344 | tf_op jit(solution)/shard_map/ppermute | solution.py:896
  149.8 0.7 broadcast_in_dim.32.mask
  150.5 0.7 broadcast_in_dim.31.instr
  151.1 88.6 %shard_map.385 = (bf16[1944,512]{1,0:T(8,128)(2,1)}, bf16[1024,512]{1,0:T(8,128)(2,1)}, bf16[2,512,1280]{2,1,0:T(8,128)(2,1)}, bf16[2,512,1024]{2,1,0:T(8,128)(2,1)}, f32[16,128]{1,0:T(8,128)}) custom-call(s32[1]{0:T(128)} %bitcast.core_ref, f32[1944,512]{1,0:T(8,128)} %get-tuple-element.50.own, f32[1944,512]{1,0:T(8,128)} %collective-permute-done.other, ...), custom_call_target="tpu_custom_call" | custom-call | tf_op jit(solution)/shard_map/pallas_call | solution.py:829
  239.7 37.4 %shard_map.386 = (bf16[64,24,512]{2,1,0:T(8,128)(2,1)}, bf16[64,24,512]{2,1,0:T(8,128)(2,1)}, f32[9,1536]{1,0:T(8,128)}) custom-call(bf16[1944,512]{1,0:T(8,128)(2,1)} %reshape.130.frames.cells, bf16[1944,512]{1,0:T(8,128)(2,1)} %get-tuple-element.56.grads, bf16[64,24,512]{2,1,0:T(8,128)(2,1)} %bitcast.93, f32[9,1536]{1,0:T(8,128)} %reshape.134.taps, ...), custom_call_target="tpu_custom_call" | custom-call | tf_op jit(solution)/shard_map/pallas_call | solution.py:519
  277.1 0.9 convert_element_type.60
  278.0 0.2 reshape.140
  278.3 0.1 copy.78
  278.4 0.8 pad.24.clone
  279.2 0.0 copy-start.21
  279.2 0.0 copy-start.22
  279.2 0.0 copy-start.13
  279.2 0.0 copy-start.1
  279.2 70.0 %shard_map.387 = (f32[24,128]{1,0:T(8,128)}, f32[24,512]{1,0:T(8,128)}, f32[24,512]{1,0:T(8,128)}, f32[16,128]{1,0:T(8,128)}, f32[16,512]{1,0:T(8,128)}, /*index=5*/f32[16,1280]{1,0:T(8,128)}, f32[16,1024]{1,0:T(8,128)}) custom-call(f32[16,128]{1,0:T(8,128)} %get-tuple-element.55.refs_0_, bf16[2,4,4,2,24,512]{5,4,3,2,1,0:T(8,128)(2,1)} %bitcast.101, ...), custom_call_target="tpu_custom_call" | custom-call | tf_op jit(solution)/shard_map/pallas_call | solution.py:313
  349.3 0.0 copy-start.9
  349.3 0.0 copy-start.6
  349.3 0.0 copy-start.7
  349.4 1.5 slice_reduce_fusion
  352.9 0.8 slice_bitcast_fusion.3
  353.7 0.8 slice_multiply_fusion
  354.5 0.1 mul.377
  354.6 0.2 copy_subtract_fusion
  354.8 0.7 copy.73
  355.4 0.7 copy.74
  356.1 0.7 copy.75
  356.8 0.8 broadcast_multiply_fusion
  357.6 0.8 fusion.28
  358.4 0.8 copy.67
  359.9 1.4 multiply_subtract_fusion.4
  361.3 0.7 multiply_subtract_fusion.1
  362.0 0.8 multiply_subtract_fusion
  362.8 0.7 multiply_subtract_fusion.2
  363.5 0.7 multiply_subtract_fusion.3
  (53 shorter events, 0.2 us)
Async XLA Ops:
  0.7 142.0 %copy-start = (s32[48,11]{0,1:T(8,128)S(1)}, s32[48,11]{0,1:T(8,128)}, u32[]{:S(2)}) copy-start(s32[48,11]{0,1:T(8,128)} %param.27) | copy-start | bytes 6340
  113.4 2.0 copy-start.5
  116.3 26.5 %copy-start.23 = (s32[8]{0:T(128)S(1)}, s32[8]{0:T(128)}, u32[]{:S(2)}) copy-start(s32[8]{0:T(128)} %param.26) | copy-start | bytes 100
  116.3 28.1 %copy-start.24 = (s32[48]{0:T(128)S(1)}, s32[48]{0:T(128)}, u32[]{:S(2)}) copy-start(s32[48]{0:T(128)} %param.28) | copy-start | bytes 580
  142.5 7.3 %collective-permute-start = (f32[1944,512]{1,0:T(8,128)}, f32[1944,512]{1,0:T(8,128)}, u32[]{:S(2)}, u32[]{:S(2)}) collective-permute-start(f32[1944,512]{1,0:T(8,128)} %get-tuple-element.50.own), channel_id=1, source_target_pairs={{0,1},{1,0},{2,3},{3,2},{4,5},{5,4},{6,7},{7,6},{8,9},{9,8},{10,11... | collective-permute-start | bytes 11943944 | tf_op jit(solution)/shard_map/ppermute | solution.py:896
  279.1 75.4 %copy-start.3 = (f32[16,11,64]{2,0,1:T(8,128)S(1)}, f32[16,11,64]{2,0,1:T(8,128)}, u32[]{:S(2)}) copy-start(f32[16,11,64]{2,0,1:T(8,128)} %param.45) | copy-start | bytes 135172
  279.1 75.4 %copy-start.10 = (f32[16,11,64]{2,0,1:T(8,128)S(1)}, f32[16,11,64]{2,0,1:T(8,128)}, u32[]{:S(2)}) copy-start(f32[16,11,64]{2,0,1:T(8,128)} %param.47) | copy-start | bytes 135172
  279.1 75.5 %copy-start.11 = (f32[16,11,64]{2,0,1:T(8,128)S(1)}, f32[16,11,64]{2,0,1:T(8,128)}, u32[]{:S(2)}) copy-start(f32[16,11,64]{2,0,1:T(8,128)} %param.46) | copy-start | bytes 135172
  279.2 80.8 %copy-start.20 = (f32[11,4]{0,1:T(4,128)S(1)}, f32[11,4]{0,1:T(4,128)}, u32[]{:S(2)}) copy-start(f32[11,4]{0,1:T(4,128)} %param.36) | copy-start | bytes 532
  279.2 80.8 %copy-start.21 = (f32[11,4]{0,1:T(4,128)S(1)}, f32[11,4]{0,1:T(4,128)}, u32[]{:S(2)}) copy-start(f32[11,4]{0,1:T(4,128)} %param.38) | copy-start | bytes 532
  279.2 80.8 %copy-start.22 = (f32[11,4]{0,1:T(4,128)S(1)}, f32[11,4]{0,1:T(4,128)}, u32[]{:S(2)}) copy-start(f32[11,4]{0,1:T(4,128)} %param.37) | copy-start | bytes 532
  279.2 82.1 %copy-start.4 = (f32[2,16,512]{2,1,0:T(8,128)S(1)}, f32[2,16,512]{2,1,0:T(8,128)}, u32[]{:S(2)}) copy-start(f32[2,16,512]{2,1,0:T(8,128)} %param.42) | copy-start | bytes 196612
  279.2 82.1 %copy-start.12 = (f32[2,16,512]{2,1,0:T(8,128)S(1)}, f32[2,16,512]{2,1,0:T(8,128)}, u32[]{:S(2)}) copy-start(f32[2,16,512]{2,1,0:T(8,128)} %param.44) | copy-start | bytes 196612
  279.2 82.1 %copy-start.13 = (f32[2,16,512]{2,1,0:T(8,128)S(1)}, f32[2,16,512]{2,1,0:T(8,128)}, u32[]{:S(2)}) copy-start(f32[2,16,512]{2,1,0:T(8,128)} %param.43) | copy-start | bytes 196612
  279.2 84.9 %copy-start.1 = (s32[48,11]{0,1:T(8,128)S(1)}, s32[48,11]{0,1:T(8,128)}, u32[]{:S(2)}) copy-start(s32[48,11]{0,1:T(8,128)} %param.27) | copy-start | bytes 6340
  349.2 12.8 %copy-start.2 = (f32[1033,24]{0,1:T(8,128)S(1)}, f32[1033,24]{0,1:T(8,128)}, u32[]{:S(2)}) copy-start(f32[1033,24]{0,1:T(8,128)} %param.30) | copy-start | bytes 297508
  349.3 12.8 %copy-start.8 = (f32[1033,24]{0,1:T(8,128)S(1)}, f32[1033,24]{0,1:T(8,128)}, u32[]{:S(2)}) copy-start(f32[1033,24]{0,1:T(8,128)} %param.32) | copy-start | bytes 297508
  349.3 12.7 %copy-start.9 = (f32[1033,24]{0,1:T(8,128)S(1)}, f32[1033,24]{0,1:T(8,128)}, u32[]{:S(2)}) copy-start(f32[1033,24]{0,1:T(8,128)} %param.31) | copy-start | bytes 297508
  349.3 12.7 %copy-start.14 = (f32[24,512]{1,0:T(8,128)S(1)}, f32[24,512]{1,0:T(8,128)}, u32[]{:S(2)}) copy-start(f32[24,512]{1,0:T(8,128)} %get-tuple-element.66) | copy-start | bytes 147460
  349.3 12.7 %copy-start.15 = (f32[24,512]{1,0:T(8,128)S(1)}, f32[24,512]{1,0:T(8,128)}, u32[]{:S(2)}) copy-start(f32[24,512]{1,0:T(8,128)} %get-tuple-element.67) | copy-start | bytes 147460
  349.3 13.5 %copy-start.6 = (f32[4,16,128]{2,1,0:T(8,128)S(1)}, f32[4,16,128]{2,1,0:T(8,128)}, u32[]{:S(2)}) copy-start(f32[4,16,128]{2,1,0:T(8,128)} %param.39) | copy-start | bytes 98308
  349.3 13.5 %copy-start.16 = (f32[4,16,128]{2,1,0:T(8,128)S(1)}, f32[4,16,128]{2,1,0:T(8,128)}, u32[]{:S(2)}) copy-start(f32[4,16,128]{2,1,0:T(8,128)} %param.41) | copy-start | bytes 98308
  349.3 13.5 %copy-start.17 = (f32[4,16,128]{2,1,0:T(8,128)S(1)}, f32[4,16,128]{2,1,0:T(8,128)}, u32[]{:S(2)}) copy-start(f32[4,16,128]{2,1,0:T(8,128)} %param.40) | copy-start | bytes 98308
  349.3 14.1 %copy-start.7 = (f32[1770,4]{0,1:T(4,128)S(1)}, f32[1770,4]{0,1:T(4,128)}, u32[]{:S(2)}) copy-start(f32[1770,4]{0,1:T(4,128)} %param.33) | copy-start | bytes 84964
  349.3 14.1 %copy-start.18 = (f32[1770,4]{0,1:T(4,128)S(1)}, f32[1770,4]{0,1:T(4,128)}, u32[]{:S(2)}) copy-start(f32[1770,4]{0,1:T(4,128)} %param.35) | copy-start | bytes 84964
  349.4 14.1 %copy-start.19 = (f32[1770,4]{0,1:T(4,128)S(1)}, f32[1770,4]{0,1:T(4,128)}, u32[]{:S(2)}) copy-start(f32[1770,4]{0,1:T(4,128)} %param.34) | copy-start | bytes 84964
where the time goes:
time: 369 us; the launch traced here: 366 us
  Pallas kernels  322 us (87%)
  local copies, waits for them, and re-layouts  19.2 us (5%)
  other arithmetic  13.1 us (4%)
  between operations  6.81 us (2%)
  waiting for transfers between devices  5.27 us (1%)
    pallas_call x1, Pallas kernels, gather_all(): pl.pallas_call(functools.partial(gather_kernel, plan), out_shape=outs, in...  99.7 us
    pallas_call x1, Pallas kernels, middle(): pl.pallas_call(middle_kernel, out_shape=[jax.ShapeDtypeStruct((PIX * PAIR...  88.6 us
    pallas_call x1, Pallas kernels, scatter_all(): pl.pallas_call(functools.partial(scatter_kernel, plan), out_shape=outs, i...  70 us
    pallas_call x1, Pallas kernels, conv_backward(): pl.pallas_call(backward_kernel, grid=(steps,), out_shape=[owned, owned, j...  37.4 us
    pallas_call x1, Pallas kernels, conv_forward(): pl.pallas_call(forward_kernel, grid=(steps,), out_shape=[kept, kept, jax....  26.2 us
  transfers between devices with their start and end apart: 1, of which 1 were waited for; matrix products, arithmetic and copies ran while one was open for 0% of the time, Pallas kernels for 0%

commit v1 on v0

v1 whole, which is shorter than its diff:
```python
import functools
import math

import jax
import jax.numpy as jnp
from jax import lax
from jax.experimental import pallas as pl
from jax.experimental.pallas import tpu as pltpu
from jax.sharding import Mesh
from jax.sharding import PartitionSpec as P

f32 = jnp.float32
bf16 = jnp.bfloat16
NAMES = ("dp_0", "dp_1", "dp_2", "mp_0", "mp_1")
SIZES = {"l": 2, "z": 4, "x": 4, "h": 2, "c": 2}
RING = 4
MESH_ID = pl.DeviceIdType.MESH
ANY = pl.BlockSpec(memory_space=pl.ANY)
INVMEM = pl.BlockSpec(memory_space=pltpu.VMEM)


def here():
    low, z, x, high, core = (lax.axis_index(n) for n in NAMES)
    return {"x": x, "y": high * 2 + low, "z": z, "c": core}


def ring(at, step):
    return lax.rem(at + step + RING, RING)


def device_of(axis, at):
    if axis == "y":
        return {"dp_0": lax.rem(at, 2), "mp_0": at // 2}
    return {{"x": "dp_2", "z": "dp_1", "c": "mp_1"}[axis]: at}


def extents(dims, at):
    found = []
    for d in dims:
        if d in at:
            v = at[d]
        elif d == "l" and "y" in at:
            v = lax.rem(at["y"], 2)
        elif d == "h" and "y" in at:
            v = at["y"] // 2
        else:
            v = (0, SIZES[d])
        found.append(v if isinstance(v, tuple) else (v, None))
    return found


def spot(dims, at):
    return tuple(start if size is None else pl.ds(start, size) for start, size in extents(dims, at))


def free_sizes(dims, at):
    return tuple(size for _, size in extents(dims, at) if size is not None)


def half(axis, side):
    return {"h": side} if axis == "y" else {axis: (2 * side, 2)}


def without(dims, axis):
    return tuple(d for d in dims if d not in ("lh" if axis == "y" else axis))


def lead(dims):
    return tuple(SIZES[d] for d in dims)


def greet(me):
    barrier = pltpu.get_barrier_semaphore()
    for axis in "xyz":
        for k in range(1, RING):
            pl.semaphore_signal(barrier, inc=1, device_id=device_of(axis, ring(me[axis], k)), device_id_type=MESH_ID)
    pl.semaphore_signal(barrier, inc=1, device_id=device_of("c", 1 - me["c"]), device_id_type=MESH_ID)
    pl.semaphore_wait(barrier, 10)


def remote(src, dst, send, recv, axis, at):
    copy = pltpu.make_async_remote_copy(
        src_ref=src, dst_ref=dst, send_sem=send, recv_sem=recv, device_id=device_of(axis, at), device_id_type=MESH_ID
    )
    copy.start()
    return copy


class Gather:
    def __init__(self, me, dims, order, shard, out, send, recv, fsend, frecv, local):
        self.me, self.dims, self.order, self.shard, self.out = me, dims, order, shard, out
        self.send, self.recv, self.fsend, self.frecv, self.local = send, recv, fsend, frecv, local
        self.forwards = []

    def region(self, phase, step=0, part=None):
        at = {a: self.me[a] for a in self.order[phase:]}
        at[self.order[phase]] = ring(self.me[self.order[phase]], step)
        if "c" in self.dims:
            at["c"] = self.me["c"]
        if part is not None:
            at.update(half(self.order[0], part))
        return self.out.at[spot(self.dims, at)]

    def push(self, phase, slot, where, step):
        axis = self.order[phase]
        src = self.shard if phase == 0 else where
        return remote(src, where, self.send.at[phase, slot], self.recv.at[phase, slot], axis, ring(self.me[axis], step))

    def forward(self, number, where):
        if "c" in self.dims:
            self.forwards.append(
                remote(where, where, self.fsend.at[number], self.frecv.at[number], "c", 1 - self.me["c"])
            )

    def begin(self):
        self.kept = pltpu.make_async_copy(self.shard, self.region(0), self.local)
        self.kept.start()
        self.launch(0)

    def launch(self, phase):
        where = self.region(phase)
        self.going = [self.push(phase, 0, where, 1), self.push(phase, 1, where, -1)]
        if phase == 0:
            self.going.append(self.push(0, 2, where, 2))

    def relay(self, phase):
        for slot, step in ((0, 1), (1, -1)):
            self.going[slot].wait()
            if phase > 0:
                self.going.append(self.push(phase, 2 + slot, self.region(phase, -step, slot), step))
                self.forward(3 * phase - 2 + slot, self.region(phase, -step))

    def finish(self, phase):
        for copy in self.going[2:]:
            copy.wait()
        if phase == 0:
            self.kept.wait()
            if "c" in self.dims:
                at = {a: self.me[a] for a in (*self.order[1:], "c")}
                self.forward(0, self.out.at[spot(self.dims, at)])
        else:
            self.forward(3 * phase, self.region(phase, 2))
        if phase < 2:
            self.launch(phase + 1)

    def end(self):
        for copy in self.forwards:
            copy.wait()


def add_into(full, dims, at, others):
    found = extents(dims, at)
    sizes = free_sizes(dims, at)

    def one(i, _):
        index, place = [], []
        for start, size in reversed(found):
            if size is None:
                index.append(start)
            else:
                index.append(start + lax.rem(i, size))
                place.append(lax.rem(i, size))
                i = i // size
        index, place = tuple(reversed(index)), tuple(reversed(place))
        total = full[index].astype(f32)
        for o in others:
            total = total + o[place].astype(f32)
        full[index] = total.astype(full.dtype)
        return 0

    lax.fori_loop(0, math.prod(sizes), one, 0)


def folded(v):
    total = None
    for r in range(0, v.shape[0], 8):
        for c in range(0, v.shape[1], 128):
            part = v[r : r + 8, c : c + 128]
            total = part if total is None else total + part
    return total


class Scatter:
    def __init__(self, me, dims, order, part, full, boxes, send, recv, local):
        self.me, self.dims, self.order, self.part, self.full, self.boxes = me, dims, order, part, full, boxes
        self.send, self.recv, self.local = send, recv, local

    def at(self, phase, step, side=None):
        at = {a: self.me[a] for a in self.order[:phase]}
        axis = self.order[phase]
        at[axis] = ring(self.me[axis], step)
        if side is not None:
            at.update(half(self.order[phase + 1], side))
        return at

    def push(self, phase, slot, src, step):
        axis = self.order[phase]
        return remote(
            src, self.boxes[phase][slot], self.send.at[phase, slot], self.recv.at[phase, slot], axis, ring(self.me[axis], step)
        )

    def begin(self):
        self.kept = pltpu.make_async_copy(self.part, self.full, self.local)
        self.kept.start()
        self.launch(0)

    def launch(self, phase):
        src = self.part if phase == 0 else self.full
        if phase < 2:
            self.going = [
                self.push(phase, side, src.at[spot(self.dims, self.at(phase, 2, side))], 1 - 2 * side) for side in range(2)
            ]
        else:
            self.going = [
                self.push(phase, slot, src.at[spot(self.dims, self.at(phase, step))], step)
                for slot, step in ((0, 2), (2, 1), (3, -1))
            ]

    def relay(self, phase):
        if phase == 0:
            self.kept.wait()
        if phase == 2:
            return
        for side, step in ((0, 1), (1, -1)):
            self.going[side].wait()
            add_into(self.full, self.dims, self.at(phase, step, side), [self.boxes[phase][side]])
            self.going.append(self.push(phase, 2 + side, self.full.at[spot(self.dims, self.at(phase, step))], step))

    def finish(self, phase):
        if phase < 2:
            for copy in self.going[2:]:
                copy.wait()
            add_into(self.full, self.dims, self.at(phase, 0), self.boxes[phase][2:4])
            self.launch(phase + 1)
            return None
        for copy in self.going:
            copy.wait()
        total = self.full[spot(self.dims, self.at(2, 0))].astype(f32)
        for slot in (0, 2, 3):
            total = total + self.boxes[2][slot][...].astype(f32)
        return total

    @staticmethod
    def scratch(dims, order, slab, dtype):
        shapes = [(*lead(dims), *slab)]
        rest = dims
        for phase, axis in enumerate(order):
            rest = without(rest, axis)
            if phase < 2:
                small = free_sizes(rest, half(order[phase + 1], 0))
            else:
                small = ()
            shapes += [(*small, *slab)] * 2 + [(*lead(rest), *slab)] * 2
        return [pltpu.VMEM(s, dtype) for s in shapes]


OWNED = ("x", "l", "z", "h")
GATHER = (
    (OWNED, ("z", "y", "x")),
    (OWNED, ("y", "z", "x")),
    (OWNED, ("z", "y", "x")),
    (("c", "l", "z", "x", "h"), ("x", "y", "z")),
    (("h", "c", "l", "z", "x"), ("x", "z", "y")),
    (("h", "c", "l", "z", "x"), ("x", "y", "z")),
)
SCATTER = (
    (OWNED, ("z", "y", "x")),
    (OWNED, ("y", "z", "x")),
    (OWNED, ("z", "y", "x")),
    (("l", "z", "x", "h"), ("z", "y", "x")),
    (("h", "l", "z", "x"), ("x", "y", "z")),
    (("h", "l", "z", "x"), ("y", "x", "z")),
)


D, EXP, MAP, PIX = 512, 3072, 9, 81
PAIR = 24
WIDTH = 384
OWNERS = WIDTH // 24
CHUNK = 3
SPAN = CHUNK * MAP * PAIR
EXPAND = 8.0 / math.sqrt(D)
PROJECT = 8.0 / math.sqrt(EXP)
VMEM_BYTES = 60 * 2**20


def sigmoid(v):
    return 0.5 + 0.5 * jnp.tanh(0.5 * v)


def nt(left, right):
    return lax.dot_general(left, right, (((1,), (1,)), ((), ())), preferred_element_type=f32)


def nn(left, right):
    return lax.dot_general(left, right, (((1,), (0,)), ((), ())), preferred_element_type=f32)


def tn(left, right):
    return lax.dot_general(left, right, (((0,), (0,)), ((), ())), preferred_element_type=f32)


def clear_borders(padded):
    zero = jnp.zeros((MAP, PAIR, WIDTH), f32)
    padded[0] = zero
    padded[MAP + 1] = zero


def each_block(body):
    def one(row, _):
        for lane in range(WIDTH // 128):
            for group in range(PAIR // 8):
                body(row, slice(8 * group, 8 * group + 8), slice(128 * lane, 128 * lane + 128))
        return 0

    lax.fori_loop(0, MAP, one, 0)


INSTR, DIMS, BINS, NTOK, FRAMES, HEADS, HD = 744, 11, 256, 8, 6, 8, 64
TABLE = INSTR + 2
ROWS = PAIR * NTOK
SMALL_AT = TABLE - D
LN_EPS = 1e-06
OUT_MULT = 2.0
HIGH = lax.Precision.HIGHEST
FILM = 16.0 / math.sqrt(D)
LEARN = 4.0 / math.sqrt(D)


def norm_fwd(x, gain):
    centre = x - jnp.mean(x, -1, keepdims=True)
    inverse = lax.rsqrt(jnp.mean(centre * centre, -1, keepdims=True) + LN_EPS)
    normed = centre * inverse
    return normed * (1.0 + gain), normed, inverse


def norm_back(normed, inverse, gain, grad_out):
    dnormed = grad_out * (1.0 + gain)
    grad_in = inverse * (
        dnormed
        - jnp.mean(dnormed, -1, keepdims=True)
        - normed * jnp.mean(dnormed * normed, -1, keepdims=True)
    )
    return grad_in, jnp.sum(grad_out * normed, 0, keepdims=True)


def gelu_parts(u):
    c = math.sqrt(2.0 / math.pi)
    square = u * u
    t = jnp.tanh(c * u * (1.0 + 0.044715 * square))
    half = 0.5 * (1.0 + t)
    return u * half, half + 0.5 * u * (1.0 - t * t) * c * (1.0 + 3.0 * 0.044715 * square)


def iota(shape, axis):
    return lax.broadcasted_iota(jnp.int32, shape, axis)


def shifted(v, places):
    tiles = [pltpu.roll(v[:, i : i + 128], (128 - places) % 128, 1) for i in range(0, v.shape[1], 128)]
    return jnp.concatenate(tiles, axis=1)


def only(v, first):
    place = iota(v.shape, 1) & 15
    return jnp.where((place >= first) & (place < first + 4), v, 0.0)


def place_of_feature(start, rows):
    d = iota((rows, D), 1)
    owner = d >> 2
    row = (owner & 1) * 1024 + (owner >> 1) * 16 + 12 + (d & 3)
    return (iota((rows, D), 0) + start == row).astype(bf16)


def middle_kernel(
    core_ref, part, cells, misc, one, two, instr, cam, bins, mask,
    dcells, dmisc, done_one, done_two, stats,
    y, logit, att, qkv, prob, ctx, up, hid, acc, dlog, lowgrad,
):
    core = core_ref[0]
    lanes = iota((PAIR, 128), 1)

    def chosen(tile):
        at = lanes + 128 * tile
        return ((at == instr[...]) | (at == INSTR + cam[0] + cam[1])).astype(f32)

    choose_lo = jnp.concatenate([chosen(i) for i in range(4)], axis=1).astype(bf16)
    choose_hi = jnp.concatenate([chosen(i) for i in range(4, 8)], axis=1).astype(bf16)
    flat = misc[...]
    cvec = only(shifted(nt(choose_lo, flat), 8) + shifted(nt(choose_hi, flat), 12), 0).astype(bf16).astype(f32)
    cvec_4 = shifted(cvec, 124)
    cvec_low, cvec_4_low = cvec.astype(bf16), cvec_4.astype(bf16)
    gamma = nn(cvec_low, flat) * FILM
    beta = nn(cvec_4_low, flat) * FILM
    scale = 1.0 + gamma
    pick = (iota((16, D), 1) == SMALL_AT + iota((16, D), 0)).astype(bf16)
    small = nn(nt(pick, flat).astype(bf16), place_of_feature(0, 2048))
    gains = [small[i : i + 1] for i in range(3)]
    learner = jnp.concatenate([small[3:11], jnp.zeros((120, D), f32)], axis=0)

    def feature(cell, _):
        rows = pl.ds(pl.multiple_of(cell * PAIR, PAIR), PAIR)
        v = cells[rows, :].astype(f32) + part[rows, :] * scale + beta
        y[rows, :] = v
        return 0

    lax.fori_loop(0, PIX, feature, 0)
    logit[...] = (
        lax.dot_general(y[...], learner, (((1,), (1,)), ((), ())), precision=HIGH, preferred_element_type=f32) * LEARN
    )

    def softmax_over_cells(v):
        v = v.reshape(PIX, PAIR, 128)
        e = jnp.exp(v - jnp.max(v, 0, keepdims=True))
        return e / jnp.sum(e, 0, keepdims=True)

    att[...] = softmax_over_cells(logit[...]).reshape(PIX * PAIR, 128)
    acc[...] = jnp.zeros_like(acc)
    for half in range(2):
        columns = slice(256 * half, 256 * half + 256)

        zero = jnp.zeros((PAIR, 256), f32)
        for t0 in range(0, NTOK, 4):

            def gather_some(cell, totals, t0=t0, columns=columns):
                rows = pl.ds(pl.multiple_of(cell * PAIR, PAIR), PAIR)
                a, v = att[rows, :], y[rows, columns]
                return tuple(t + a[:, t0 + i : t0 + i + 1] * v for i, t in enumerate(totals))

            totals = lax.fori_loop(0, PIX, gather_some, (zero,) * 4)
            for i in range(4):
                acc[(t0 + i) * PAIR : (t0 + i + 1) * PAIR, columns] = totals[i]
    tok = acc[...].astype(bf16).astype(f32)

    h1, normed1, inverse1 = norm_fwd(tok, gains[0])
    h1_low = h1.astype(bf16)
    row_q, row_k = iota((ROWS, ROWS), 0), iota((ROWS, ROWS), 1)
    image_q, image_k = lax.rem(row_q, PAIR), lax.rem(row_k, PAIR)
    order_q = image_q * NTOK + lax.div(row_q, PAIR)
    order_k = image_k * NTOK + lax.div(row_k, PAIR)
    seen = (lax.div(image_q, FRAMES) == lax.div(image_k, FRAMES)) & (order_k <= order_q)
    root = HD**-0.5
    acc[...] = jnp.zeros_like(acc)

    def attend(m, _):
        p = nn(h1_low, one[m, :, 0:384]).astype(bf16)
        qkv[m] = p
        outs = []
        for head in range(2):
            q, k, v = (p[:, 128 * j + 64 * head : 128 * j + 64 * head + 64] for j in range(3))
            s = jnp.where(seen, nt(q, k) * root, -1e30)
            e = jnp.exp(s - jnp.max(s, -1, keepdims=True))
            w = e / jnp.sum(e, -1, keepdims=True)
            prob[m, head] = w
            outs.append(nn(w.astype(bf16), v))
        o = jnp.concatenate(outs, axis=1).astype(bf16)
        ctx[m] = o
        acc[...] += nt(o, one[m, :, 384:512])
        return 0

    lax.fori_loop(0, 4, attend, 0)
    x1 = tok + OUT_MULT * acc[...]
    h2, normed2, inverse2 = norm_fwd(x1, gains[1])
    h2_low = h2.astype(bf16)
    acc[...] = x1

    def feed(m, _):
        u = nn(h2_low, two[m, :, 0:512])
        up[m] = u
        low = gelu_parts(u)[0].astype(bf16)
        hid[m] = low
        acc[...] += nt(low, two[m, :, 512:1024])
        return 0

    lax.fori_loop(0, 4, feed, 0)
    x2 = acc[...]
    normed_out, normed3, inverse3 = norm_fwd(x2, gains[2])
    pooled = (jnp.sum(normed_out.reshape(NTOK, PAIR, D), axis=0) * (1.0 / NTOK)).astype(bf16)

    low_half = lanes < 64
    scores = [nn(pooled, one[m, :, 512:1280]) for m in range(4)]
    weight = mask[...]
    loss = jnp.zeros((PAIR, 128), f32)
    for u in range(6):
        tiles = [s[:, 128 * u : 128 * u + 128] for s in scores]
        top = jnp.maximum(jnp.maximum(tiles[0], tiles[1]), jnp.maximum(tiles[2], tiles[3]))
        left = jnp.max(jnp.where(low_half, top, -jnp.inf), -1, keepdims=True)
        right = jnp.max(jnp.where(low_half, -jnp.inf, top), -1, keepdims=True)
        top = jnp.where(low_half, left, right)
        total = sum(jnp.exp(t - top) for t in tiles)
        left = jnp.sum(jnp.where(low_half, total, 0.0), -1, keepdims=True)
        right = jnp.sum(jnp.where(low_half, 0.0, total), -1, keepdims=True)
        lse = top + jnp.log(jnp.where(low_half, left, right))
        label = jnp.where(low_half, bins[:, 2 * u : 2 * u + 1], bins[:, 2 * u + 1 : 2 * u + 2])
        real = low_half | (2 * u + 1 < DIMS)
        target = jnp.zeros((PAIR, 128), f32)
        for m, t in enumerate(tiles):
            hit = label == (lanes & 63) + 64 * m
            target = target + jnp.where(hit, t, 0.0)
            slope = weight * (jnp.exp(t - lse) - hit.astype(f32))
            dlog[m, :, 128 * u : 128 * u + 128] = jnp.where(real, slope, 0.0).astype(bf16)
        counted = real & ((lanes & 63) == 0)
        loss = loss + weight * (jnp.where(counted, lse, 0.0) - target)
    stats[...] = jnp.zeros_like(stats)
    stats[0:8] = loss[0:8] + loss[8:16] + loss[16:24]
    counts = jnp.where(lanes == 0, weight, 0.0)
    stats[8:16] = counts[0:8] + counts[8:16] + counts[16:24]
    dpooled = jnp.zeros((PAIR, D), f32)
    for m in range(4):
        dpooled = dpooled + nt(dlog[m], one[m, :, 512:1280])
    dnormed = jnp.broadcast_to(dpooled * (1.0 / NTOK), (NTOK, PAIR, D)).reshape(ROWS, D)
    dx2, dgain2 = norm_back(normed3, inverse3, gains[2], dnormed)
    dbranch = dx2.astype(bf16)
    acc[...] = jnp.zeros_like(acc)

    def feed_back(m, _):
        slope = gelu_parts(up[m])[1]
        dup = (nn(dbranch, two[m, :, 512:1024]) * slope).astype(bf16)
        lowgrad[m] = dup
        acc[...] += nt(dup, two[m, :, 0:512])
        return 0

    lax.fori_loop(0, 4, feed_back, 0)
    dx1_norm, dgain1 = norm_back(normed2, inverse2, gains[1], acc[...])
    dx1 = dx2 + dx1_norm
    dattn = dx1.astype(bf16)

    def feed_weights(h, _):
        m = 2 * h + core
        done_one[h, :, 512:1280] = tn(pooled, dlog[m]).astype(bf16)
        done_two[h, :, 0:512] = tn(h2_low, lowgrad[m]).astype(bf16)
        done_two[h, :, 512:1024] = tn(dbranch, hid[m]).astype(bf16)
        done_one[h, :, 384:512] = (tn(dattn, ctx[m]) * OUT_MULT).astype(bf16)
        return 0

    lax.fori_loop(0, 2, feed_weights, 0)
    acc[...] = jnp.zeros_like(acc)

    def attend_back(m, _):
        do = (nn(dattn, one[m, :, 384:512]) * OUT_MULT).astype(bf16)
        p = qkv[m]
        dq, dk, dv = [], [], []
        for head in range(2):
            q, k, v = (p[:, 128 * j + 64 * head : 128 * j + 64 * head + 64] for j in range(3))
            w = prob[m, head]
            d = do[:, 64 * head : 64 * head + 64]
            dp = nt(d, v)
            dv.append(tn(w.astype(bf16), d))
            ds = (w * (dp - jnp.sum(w * dp, -1, keepdims=True))).astype(bf16)
            dq.append(nn(ds, k) * root)
            dk.append(tn(ds, q) * root)
        g = jnp.concatenate([*dq, *dk, *dv], axis=1).astype(bf16)
        lowgrad[m, :, 0:384] = g
        acc[...] += nt(g, one[m, :, 0:384])
        return 0

    lax.fori_loop(0, 4, attend_back, 0)

    def attend_weights(h, _):
        done_one[h, :, 0:384] = tn(h1_low, lowgrad[2 * h + core, :, 0:384]).astype(bf16)
        return 0

    lax.fori_loop(0, 2, attend_weights, 0)
    dtok_norm, dgain0 = norm_back(normed1, inverse1, gains[0], acc[...])
    acc[...] = dx1 + dtok_norm

    def slope_of(cell, _):
        rows = pl.ds(pl.multiple_of(cell * PAIR, PAIR), PAIR)
        v = y[rows, :]
        found = jnp.zeros((PAIR, 128), f32)
        for t in range(NTOK):
            s = jnp.sum(v * acc[t * PAIR : (t + 1) * PAIR, :], -1, keepdims=True)
            found = jnp.where(lanes == t, s, found)
        logit[rows, :] = found
        return 0

    lax.fori_loop(0, PIX, slope_of, 0)
    a = att[...].reshape(PIX, PAIR, 128)
    da = logit[...].reshape(PIX, PAIR, 128)
    logit[...] = (a * (da - jnp.sum(a * da, 0, keepdims=True)) * LEARN).reshape(PIX * PAIR, 128)
    dlearner = lax.dot_general(logit[...], y[...], (((0,), (0,)), ((), ())), precision=HIGH, preferred_element_type=f32)

    def spread(cell, sums):
        rows = pl.ds(pl.multiple_of(cell * PAIR, PAIR), PAIR)
        a, dl = att[rows, :], logit[rows, :]
        dy = jnp.zeros((PAIR, D), f32)
        for t in range(NTOK):
            dy = dy + a[:, t : t + 1] * acc[t * PAIR : (t + 1) * PAIR, :] + dl[:, t : t + 1] * learner[t : t + 1]
        dcells[rows, :] = (dy * scale).astype(bf16)
        return sums[0] + dy * part[rows, :], sums[1] + dy

    zero = jnp.zeros((PAIR, D), f32)
    dgamma, dbeta = lax.fori_loop(0, PIX, spread, (zero, zero))
    dgamma, dbeta = dgamma.astype(bf16), dbeta.astype(bf16)
    dcvec = only(nt(dgamma, flat) + shifted(nt(dbeta, flat), 4), 0) * FILM
    high = dcvec.astype(bf16).astype(f32)
    rest = dcvec - high
    dsmall = jnp.concatenate([dgain0, dgain1, dgain2, dlearner[0:8], jnp.zeros((5, D), f32)], axis=0).astype(bf16)
    mine = pl.ds(pl.multiple_of(core * 1024, 1024), 1024)
    lhs = jnp.concatenate(
        [cvec, cvec_4, shifted(high, 120), shifted(rest, 120), shifted(high, 116), shifted(rest, 116)], axis=0
    )
    lhs = jnp.where(core == 0, lhs[:, 0:1024], lhs[:, 1024:2048])
    lhs = jnp.concatenate([lhs, nt(dsmall, place_of_feature(core * 1024, 1024))], axis=0).astype(bf16)
    rhs = jnp.concatenate([dgamma, dbeta, choose_lo, choose_lo, choose_hi, choose_hi, pick], axis=0)
    result = tn(lhs, rhs)
    film_rows = (iota((1024, D), 0) & 15) < 8
    dmisc[...] = jnp.where(film_rows, result * FILM, result).astype(bf16)


def middle(core, part, cells, misc, one, two, instr, cam, bins, mask):
    vmem = pl.BlockSpec(memory_space=pltpu.VMEM)
    return pl.pallas_call(
        middle_kernel,
        out_shape=[
            jax.ShapeDtypeStruct((PIX * PAIR, D), bf16),
            jax.ShapeDtypeStruct((1024, D), bf16),
            jax.ShapeDtypeStruct((2, D, 1280), bf16),
            jax.ShapeDtypeStruct((2, D, 1024), bf16),
            jax.ShapeDtypeStruct((16, 128), f32),
        ],
        in_specs=[pl.BlockSpec(memory_space=pltpu.SMEM)] + [vmem] * 9,
        out_specs=[vmem] * 5,
        scratch_shapes=[
            pltpu.VMEM((PIX * PAIR, D), f32),
            pltpu.VMEM((PIX * PAIR, 128), f32),
            pltpu.VMEM((PIX * PAIR, 128), f32),
            pltpu.VMEM((4, ROWS, 384), bf16),
            pltpu.VMEM((4, 2, ROWS, ROWS), f32),
            pltpu.VMEM((4, ROWS, 128), bf16),
            pltpu.VMEM((4, ROWS, 512), f32),
            pltpu.VMEM((4, ROWS, 512), bf16),
            pltpu.VMEM((ROWS, D), f32),
            pltpu.VMEM((4, PAIR, 768), bf16),
            pltpu.VMEM((4, ROWS, 512), bf16),
        ],
        compiler_params=pltpu.CompilerParams(vmem_limit_bytes=VMEM_BYTES),
    )(core, part, cells, misc, one, two, instr, cam, bins, mask)


STEPS = 4
BLOCK = (PIX, PAIR, WIDTH)


def tap_places():
    row, col = iota((OWNERS * 128, WIDTH), 0), iota((OWNERS * 128, WIDTH), 1)
    return (((row >> 7) * 24 + (row & 127) == col) & ((row & 127) < 24)).astype(bf16)


def to_cells(frames, cells):
    rows = 8 * PAIR
    at, of = iota((rows, rows), 0), iota((rows, rows), 1)
    turn = (lax.rem(at, PAIR) * 8 + lax.div(at, PAIR) == of).astype(bf16)
    for first in (*range(0, PIX - 8, 8), PIX - 8):
        block = frames[:, :, first : first + 8, :].reshape(rows, D)
        cells[first * PAIR : first * PAIR + rows, :] = nn(turn, block).astype(bf16)


def forward_kernel(plan, *refs):
    n = len(plan)
    pairs, shards = refs[0:2], refs[2 : 2 + n]
    refs = refs[2 + n :]
    cam2, cells_out, project_out, taps_out, misc_out, one_out, two_out, pre_out, deep_out, total_out = refs[:10]
    frames2, cells, expand, project, slabs, taps, places, act, pre, deep, part, other = refs[10:22]
    send, recv, fsend, frecv, local, kept, swap_send, swap_recv = refs[22:]
    me = here()
    greet(me)
    swaps = []
    for i, out in enumerate((frames2, cam2)):
        mine = pltpu.make_async_copy(pairs[i], out.at[me["c"]], local.at[n + i])
        mine.start()
        swaps += [mine, remote(pairs[i], out.at[me["c"]], swap_send.at[i], swap_recv.at[i], "c", 1 - me["c"])]
    outs = (expand, project, slabs, misc_out, one_out, two_out)
    jobs = [
        Gather(me, dims, order, shards[b], outs[b], send.at[b], recv.at[b], fsend.at[b], frecv.at[b], local.at[b])
        for b, (dims, order) in enumerate(plan)
    ]
    first, rest = jobs[:3], jobs[3:]

    def relay(some, phase):
        for job in some:
            job.relay(phase)

    def finish(some, phase):
        for job in some:
            job.finish(phase)

    for job in jobs:
        job.begin()
    clear_borders(act)
    part[...] = jnp.zeros_like(part)
    places[...] = tap_places()
    relay(first, 0)
    finish(first, 0)
    swaps[0].wait()
    swaps[1].wait()
    to_cells(frames2, cells)
    relay(first, 1)
    finish(first, 1)
    relay(rest, 0)
    finish(rest, 0)
    saves = []

    def save(src, dst, number):
        copy = pltpu.make_async_copy(src, dst, kept.at[number])
        copy.start()
        saves.append(copy)

    save(cells, cells_out, 0)
    spans = [None] * STEPS
    for step in range(STEPS):
        slot = step % 2
        at = ring(me["x"], (0, -1, 1, 2)[step])
        if step == 1:
            relay(first, 2)
        if step == 3:
            finish(first, 2)
            save(project, project_out, 1)
        if step >= 2:
            for copy in spans[step - 2]:
                copy.wait()
        weight = expand[at].reshape(WIDTH, D)
        back = project[at].reshape(WIDTH, D)
        tap = slabs[at].reshape(OWNERS, 16, 128)
        side = jnp.concatenate([tap[i] for i in range(OWNERS)], axis=1)
        taps[at] = nn(side, places[...]) * (8.0 / 3.0)

        def enter(i, _, weight=weight, slot=slot):
            rows = pl.ds(pl.multiple_of(i * SPAN, SPAN), SPAN)
            e = (nt(cells[rows, :], weight) * EXPAND).reshape(CHUNK * MAP, PAIR, WIDTH)
            pre[slot, pl.ds(i * CHUNK * MAP, CHUNK * MAP)] = e
            act[pl.ds(1 + i * CHUNK, CHUNK)] = (e * sigmoid(e)).reshape(CHUNK, MAP, PAIR, WIDTH)
            return 0

        lax.fori_loop(0, MAP // CHUNK, enter, 0)
        out = [pltpu.make_async_copy(pre.at[slot], pre_out.at[at], kept.at[3 + 2 * step])]
        out[0].start()
        if step == 0:
            relay(rest, 1)
        if step == 2:
            relay(rest, 2)

        def mix(row, subs, cols, slot=slot, at=at):
            near = act[pl.ds(row, 3), :, subs, cols]
            tap = [jnp.broadcast_to(taps[at, t : t + 1, cols], (8, 128)) for t in range(9)]
            for col in range(MAP):
                total = None
                for t in range(9):
                    p = col + t % 3 - 1
                    if 0 <= p < MAP:
                        term = near[t // 3, p] * tap[t]
                        total = term if total is None else total + term
                deep[slot, row * MAP + col, subs, cols] = total

        each_block(mix)
        out.append(pltpu.make_async_copy(deep.at[slot], deep_out.at[at], kept.at[4 + 2 * step]))
        out[1].start()
        spans[step] = out
        if step == 0:
            finish(rest, 1)
        if step == 3:
            finish(rest, 2)

        def leave(i, _, back=back, slot=slot):
            rows = pl.ds(pl.multiple_of(i * SPAN, SPAN), SPAN)
            v = deep[slot, pl.ds(i * CHUNK * MAP, CHUNK * MAP)].reshape(SPAN, WIDTH)
            part[rows, :] += nn((v * sigmoid(v)).astype(bf16), back) * PROJECT
            return 0

        if step < STEPS - 1:
            lax.fori_loop(0, MAP // CHUNK, leave, 0)
    save(taps, taps_out, 2)
    trades = []
    for i in range(MAP // CHUNK):
        leave(i, 0)
        rows = pl.ds(i * SPAN, SPAN)
        trades.append(
            remote(part.at[rows], other.at[rows], swap_send.at[2 + i], swap_recv.at[2 + i], "c", 1 - me["c"])
        )
    for i, copy in enumerate(trades):
        copy.wait()
        rows = slice(i * SPAN, (i + 1) * SPAN)
        other[rows, :] += part[rows, :]
        save(other.at[rows], total_out.at[rows], 3 + 2 * STEPS + i)
    for step in (STEPS - 2, STEPS - 1):
        saves += spans[step]
    for job in jobs:
        job.end()
    for copy in saves + swaps[2:]:
        copy.wait()


def forward(pairs, shards, plan, collective_id):
    n = len(plan)
    frames, cam = pairs
    maps = jax.ShapeDtypeStruct((STEPS, *BLOCK), f32)
    shape = jax.ShapeDtypeStruct
    full = [shape((*lead(dims), *s.shape), s.dtype) for s, (dims, _) in zip(shards, plan)]
    rows = PIX * PAIR
    return pl.pallas_call(
        functools.partial(forward_kernel, plan),
        out_shape=[
            shape((2, *cam.shape), cam.dtype),
            shape((rows, D), bf16),
            full[1],
            shape((STEPS, 16, WIDTH), f32),
            *full[3:],
            maps,
            maps,
            shape((rows, D), f32),
        ],
        in_specs=[ANY] * (2 + n),
        out_specs=[ANY] * 10,
        scratch_shapes=[
            pltpu.VMEM((2, *frames.shape), bf16),
            pltpu.VMEM((rows, D), bf16),
            pltpu.VMEM(full[0].shape, bf16),
            pltpu.VMEM(full[1].shape, bf16),
            pltpu.VMEM(full[2].shape, bf16),
            pltpu.VMEM((STEPS, 16, WIDTH), f32),
            pltpu.VMEM((OWNERS * 128, WIDTH), bf16),
            pltpu.VMEM((MAP + 2, MAP, PAIR, WIDTH), f32),
            pltpu.VMEM((2, *BLOCK), f32),
            pltpu.VMEM((2, *BLOCK), f32),
            pltpu.VMEM((rows, D), f32),
            pltpu.VMEM((rows, D), f32),
            pltpu.SemaphoreType.DMA((n, 3, 4)),
            pltpu.SemaphoreType.DMA((n, 3, 4)),
            pltpu.SemaphoreType.DMA((n, 7)),
            pltpu.SemaphoreType.DMA((n, 7)),
            pltpu.SemaphoreType.DMA((n + 2,)),
            pltpu.SemaphoreType.DMA((3 + 2 * STEPS + MAP // CHUNK,)),
            pltpu.SemaphoreType.DMA((2 + MAP // CHUNK,)),
            pltpu.SemaphoreType.DMA((2 + MAP // CHUNK,)),
        ],
        compiler_params=pltpu.CompilerParams(
            collective_id=collective_id, has_side_effects=True, vmem_limit_bytes=VMEM_BYTES
        ),
    )(*pairs, *shards)


class Blocks:
    def __init__(self, me, dims, order, full, room, send, recv):
        self.me, self.dims, self.order, self.full = me, dims, order, full
        self.halves, self.wholes, self.slabs, self.last = room
        self.send, self.recv = send, recv
        self.going = [None] * STEPS
        self.sent = []

    def at(self, step, **more):
        return {"x": ring(self.me["x"], BACK[step]), **more}

    def push(self, step, slot, src, box, axis, move):
        return remote(src, box, self.send.at[step, slot], self.recv.at[step, slot], axis, ring(self.me[axis], move))

    def launch(self, step):
        a, b, _ = self.order
        self.going[step] = [
            self.push(
                step, side, self.full.at[spot(self.dims, self.at(step, **{a: ring(self.me[a], 2)}, **half(b, side)))],
                self.halves.at[step, side], a, 1 - 2 * side,
            )
            for side in range(2)
        ]

    def relay(self, step):
        a, b, _ = self.order
        for side, move in ((0, 1), (1, -1)):
            self.going[step][side].wait()
            pos = {a: ring(self.me[a], move)}
            add_into(self.full, self.dims, self.at(step, **pos, **half(b, side)), [self.halves.at[step, side]])
            where = self.full.at[spot(self.dims, self.at(step, **pos))]
            self.going[step].append(self.push(step, 2 + side, where, self.wholes.at[step, side], a, move))

    def middle(self, step):
        a, b, _ = self.order
        for copy in self.going[step][2:]:
            copy.wait()
        own = {a: self.me[a]}
        add_into(self.full, self.dims, self.at(step, **own), [self.wholes.at[step, side] for side in range(2)])
        self.going[step] = [
            self.push(
                step, 4 + i, self.full.at[spot(self.dims, self.at(step, **own, **{b: ring(self.me[b], move)}))],
                self.slabs.at[step, i], b, move,
            )
            for i, move in enumerate((2, 1, -1))
        ]

    def finish(self, step):
        a, b, _ = self.order
        for copy in self.going[step]:
            copy.wait()
        index = spot(self.dims, self.at(step, **{a: self.me[a], b: self.me[b]}))
        total = self.full[index].astype(f32)
        for i in range(3):
            total = total + self.slabs[step, i].astype(f32)
        if BACK[step] != 0:
            self.full[index] = total.astype(bf16)
            self.sent.append(self.push(step, 7, self.full.at[index], self.last.at[step], "x", BACK[step]))
        return total

    def close(self, total):
        for copy in self.sent:
            copy.wait()
        for i in range(STEPS - 1):
            total = total + self.last[i].astype(f32)
        return total

    @staticmethod
    def scratch(dims, order, slab):
        rest = without(without(dims, "x"), order[0])
        small = free_sizes(rest, half(order[1], 0))
        shapes = [
            (*lead(dims), *slab), (STEPS, 2, *small, *slab), (STEPS, 2, *lead(rest), *slab), (STEPS, 3, *slab),
            (STEPS - 1, *slab),
        ]
        return [pltpu.VMEM(s, bf16) for s in shapes]


BACK = (2, 1, -1, 0)


def backward_kernel(plan, *refs):
    n = len(plan)
    cells_in, dcells_in, project_in, taps_in, pre_in, deep_in, stats = refs[:7]
    parts = refs[7 : 7 + n - 3]
    refs = refs[4 + n :]
    stats_out, outs = refs[0], refs[1 : 1 + n]
    refs = refs[1 + n :]
    cells, dcells, project, taps, places, pre, deep, spread, mid, dpre, acc = refs[:11]
    refs = refs[11:]
    blocks_room, rest_room = refs[:15], refs[15 : 15 + 13 * (n - 3)]
    tile, tile_box, bsend, brecv, send, recv, local, kept, tsend, trecv = refs[15 + 13 * (n - 3) :]
    me = here()
    loads = []
    for i, (src, dst) in enumerate(((cells_in, cells), (dcells_in, dcells), (project_in, project), (taps_in, taps))):
        copy = pltpu.make_async_copy(src, dst, kept.at[i])
        copy.start()
        loads.append(copy)

    def fetch(step):
        at = ring(me["x"], BACK[step])
        pair = []
        for i, (src, dst) in enumerate(((pre_in, pre), (deep_in, deep))):
            copy = pltpu.make_async_copy(src.at[at], dst.at[step % 2], kept.at[4 + 2 * step + i])
            copy.start()
            pair.append(copy)
        return pair

    maps = [fetch(0), fetch(1), None, None]
    greet(me)
    rest = []
    for b, (dims, order) in enumerate(plan[3:]):
        own = rest_room[13 * b : 13 * b + 13]
        boxes = [own[1:5], own[5:9], own[9:13]]
        rest.append(Scatter(me, dims, order, parts[b], own[0], boxes, send.at[b], recv.at[b], local.at[b]))
    first = [
        Blocks(me, dims, order, blocks_room[5 * b], blocks_room[5 * b + 1 : 5 * b + 5], bsend.at[b], brecv.at[b])
        for b, (dims, order) in enumerate(plan[:3])
    ]
    for job in rest:
        job.begin()
    clear_borders(spread)
    places[...] = tap_places()
    for copy in loads:
        copy.wait()
    square = jnp.zeros((8, 128), f32)

    def close_rest(square):
        for b, job in enumerate(rest):
            total = job.finish(2)
            outs[3 + b][...] = total
            square = square + folded(total * total)
        return square

    for step in range(STEPS):
        slot = step % 2
        at = ring(me["x"], BACK[step])
        for copy in maps[step]:
            copy.wait()
        back = project[at].reshape(WIDTH, D)

        def enter(i, _, back=back, slot=slot):
            rows = pl.ds(pl.multiple_of(i * SPAN, SPAN), SPAN)
            dmid = nt(dcells[rows, :], back) * PROJECT
            v = deep[slot, pl.ds(i * CHUNK * MAP, CHUNK * MAP)].reshape(SPAN, WIDTH)
            s = sigmoid(v)
            m = v * s
            mid[rows, :] = m.astype(bf16)
            spread[pl.ds(1 + i * CHUNK, CHUNK)] = (dmid * (s + m * (1.0 - s))).reshape(CHUNK, MAP, PAIR, WIDTH)
            return 0

        lax.fori_loop(0, MAP // CHUNK, enter, 0)
        if step > 0:
            for job in first:
                job.relay(step - 1)
        if step > 1:
            for job in first:
                job.finish(step - 2)
        if step == 2:
            for job in rest:
                job.relay(1)
        if step == 3:
            square = close_rest(square)
        acc[...] = jnp.zeros_like(acc)

        def mix(row, subs, cols, slot=slot, at=at):
            near = spread[pl.ds(row, 3), :, subs, cols]
            tap = [jnp.broadcast_to(taps[at, t : t + 1, cols], (8, 128)) for t in range(9)]
            sums = [None] * 9
            for col in range(MAP):
                e = pre[slot, row * MAP + col, subs, cols]
                s = sigmoid(e)
                a = e * s
                total = None
                for t in range(9):
                    p = col + 1 - t % 3
                    if 0 <= p < MAP:
                        g = near[2 - t // 3, p]
                        term = g * tap[t]
                        total = term if total is None else total + term
                        term = g * a
                        sums[t] = term if sums[t] is None else sums[t] + term
                dpre[row * MAP + col, subs, cols] = total * (s + a * (1.0 - s))
            for t in range(9):
                acc[t, :, cols] += sums[t]

        each_block(mix)
        if step + 2 < STEPS:
            maps[step + 2] = fetch(step + 2)
        if step == 0:
            for job in rest:
                job.relay(0)
        if step == 1:
            for job in rest:
                job.finish(0)
        if step == 2:
            for job in rest:
                job.finish(1)
        if step > 0:
            for job in first:
                job.middle(step - 1)
        owned = (2, 4, 2, 24, D)
        low = dpre[...].reshape(PIX * PAIR, WIDTH).astype(bf16)
        first[0].full[at] = (tn(low, cells[...]) * EXPAND).astype(bf16).reshape(owned)
        first[1].full[at] = (tn(mid[...], dcells[...]) * PROJECT).astype(bf16).reshape(owned)
        dtaps = jnp.concatenate([jnp.sum(acc[...], axis=1) * (8.0 / 3.0), jnp.zeros((7, WIDTH), f32)], axis=0)
        side = nt(dtaps.astype(bf16), places[...]).astype(bf16)
        for i in range(OWNERS):
            first[2].full[at, i // 8, (i // 2) % 4, i % 2] = side[:, 128 * i : 128 * i + 128]
        for job in first:
            job.launch(step)
    for job in first:
        job.relay(STEPS - 1)
    for job in first:
        job.finish(STEPS - 2)
    for job in first:
        job.middle(STEPS - 1)
    for b, job in enumerate(first):
        total = job.close(job.finish(STEPS - 1))
        outs[b][...] = total
        square = square + folded(total * total)
    tile[0, 0:16, :] = stats[...]
    tile[0, 16:24, :] = square
    for phase, axis in enumerate("cxyz"):
        size = 2 if axis == "c" else RING
        copies = [
            remote(
                tile.at[phase], tile_box.at[phase, k - 1], tsend.at[phase, k - 1], trecv.at[phase, k - 1],
                axis, lax.rem(me[axis] + k, size),
            )
            for k in range(1, size)
        ]
        for copy in copies:
            copy.wait()
        total = tile[phase]
        for k in range(size - 1):
            total = total + tile_box[phase, k]
        tile[phase + 1] = total
    stats_out[...] = tile[4]


def backward(cells, dcells, project, taps, pre, deep, stats, parts, slabs, plan, collective_id):
    n = len(plan)
    shape = jax.ShapeDtypeStruct
    rows = PIX * PAIR
    room = []
    for (dims, order), slab in zip(plan[:3], slabs[:3]):
        room += Blocks.scratch(dims, order, slab)
    for (dims, order), slab in zip(plan[3:], slabs[3:]):
        room += Scatter.scratch(dims, order, slab, bf16)
    return pl.pallas_call(
        functools.partial(backward_kernel, plan),
        out_shape=[shape((24, 128), f32)] + [shape(s, f32) for s in slabs],
        in_specs=[ANY] * 6 + [INVMEM] + [ANY] * (n - 3),
        out_specs=[INVMEM] * (1 + n),
        scratch_shapes=[
            pltpu.VMEM((rows, D), bf16),
            pltpu.VMEM((rows, D), bf16),
            pltpu.VMEM(project.shape, bf16),
            pltpu.VMEM(taps.shape, f32),
            pltpu.VMEM((OWNERS * 128, WIDTH), bf16),
            pltpu.VMEM((2, *BLOCK), f32),
            pltpu.VMEM((2, *BLOCK), f32),
            pltpu.VMEM((MAP + 2, MAP, PAIR, WIDTH), f32),
            pltpu.VMEM((rows, WIDTH), bf16),
            pltpu.VMEM(BLOCK, f32),
            pltpu.VMEM((9, 8, WIDTH), f32),
            *room,
            pltpu.VMEM((5, 24, 128), f32),
            pltpu.VMEM((4, 3, 24, 128), f32),
            pltpu.SemaphoreType.DMA((3, STEPS, 8)),
            pltpu.SemaphoreType.DMA((3, STEPS, 8)),
            pltpu.SemaphoreType.DMA((n - 3, 3, 4)),
            pltpu.SemaphoreType.DMA((n - 3, 3, 4)),
            pltpu.SemaphoreType.DMA((n - 3,)),
            pltpu.SemaphoreType.DMA((4 + 2 * STEPS,)),
            pltpu.SemaphoreType.DMA((4, 3)),
            pltpu.SemaphoreType.DMA((4, 3)),
        ],
        compiler_params=pltpu.CompilerParams(
            collective_id=collective_id, has_side_effects=True, vmem_limit_bytes=VMEM_BYTES
        ),
    )(cells, dcells, project, taps, pre, deep, stats, *parts)


TAIL = TABLE + 11
IMAGES = 12
MP = ("mp_0", "mp_1")
DP_MP = NAMES
DP = ("dp_0", "dp_1", "dp_2")
CLIP_NORM = 0.02
BETA_ONE = 0.9
BETA_TWO = 0.999
ADAM_EPS = 1e-08
DECAY = 0.01
RATES = (0.1, 0.1, 0.2, 0.05, 0.05, 0.2)


def adam(master, first, second, grad, t, rate):
    first_new = BETA_ONE * first + (1.0 - BETA_ONE) * grad
    second_new = BETA_TWO * second + (1.0 - BETA_TWO) * grad * grad
    m_hat = first_new / (1.0 - BETA_ONE**t)
    v_hat = second_new / (1.0 - BETA_TWO**t)
    master_new = master - rate * (m_hat / (jnp.sqrt(v_hat) + ADAM_EPS) + DECAY * master)
    return [master_new, first_new, second_new]


def pack_misc(film, table, small):
    tail = jnp.concatenate([table, small], axis=1)
    tail = jnp.pad(tail, ((0, 0), (0, 2 * D - tail.shape[1])))
    return jnp.concatenate([film[:, :D], film[:, D:], tail[:, :D], tail[:, D:]], axis=0)


def unpack_misc(misc):
    film = jnp.concatenate([misc[0:4], misc[4:8]], axis=1)
    tail = jnp.concatenate([misc[8:12], misc[12:16]], axis=1)
    return film, tail[:, :TABLE], tail[:, TABLE:TAIL]


def pack_attn_head(attn, head):
    both = jnp.concatenate([*attn, head], axis=-1)
    return jnp.pad(both, [(0, 0)] * (both.ndim - 1) + [(0, 1280 - both.shape[-1])])


def per_device(
    frames, camera_ids, instruction_ids, action_bins, final_mask, step_count,
    conv_w, conv_m1, conv_m2, cond_w, cond_m1, cond_m2, small_w, small_m1, small_m2,
    attn_w, attn_m1, attn_m2, mlp_w, mlp_m1, mlp_m2, head_w, head_m1, head_m2,
):
    core, high = lax.axis_index("mp_1"), lax.axis_index("mp_0")
    conv_t = conv_w.T.astype(bf16)
    cond_t = cond_w.T.astype(bf16)
    attn_l = attn_w.astype(bf16)
    shards = (
        conv_t[:, :D],
        conv_t[:, D : 2 * D],
        jnp.pad(conv_w[2 * D :].astype(bf16), ((0, 7), (0, 104))),
        pack_misc(cond_t[:, : 2 * D], cond_t[:, 2 * D :], small_w.T.astype(bf16)),
        pack_attn_head([attn_l[j] for j in range(4)], head_w.astype(bf16).reshape(16, DIMS * 64)),
        jnp.moveaxis(mlp_w.astype(bf16), 0, 1).reshape(16, 1024),
    )
    image = jnp.arange(PAIR)
    cam = jnp.where(image // IMAGES == core, jnp.tile(camera_ids, 2), 0)
    cam = jnp.broadcast_to(cam[:, None], (PAIR, 128))
    cam2, cells, project, taps, misc_all, one_all, two_all, pre, deep, part = forward((frames, cam), shards, GATHER, 1)
    instr = jnp.repeat(lax.dynamic_slice_in_dim(instruction_ids, high * 4, 4), FRAMES)
    bins = jnp.pad(
        lax.dynamic_slice_in_dim(action_bins, high * PAIR, PAIR), ((0, 0), (0, 128 - DIMS)), constant_values=-1
    )
    mask = lax.dynamic_slice_in_dim(final_mask, high * PAIR, PAIR).astype(f32)
    dcells, dmisc, done_one, done_two, stats = middle(
        core[None],
        part,
        cells,
        misc_all.reshape(2048, D),
        one_all.reshape(4, D, 1280),
        two_all.reshape(4, D, 1024),
        jnp.broadcast_to(instr[:, None], (PAIR, 128)),
        cam2,
        bins,
        jnp.broadcast_to(mask[:, None], (PAIR, 128)),
    )
    parts = [
        g.reshape(*lead(dims), *s.shape)
        for g, s, (dims, _) in zip((dmisc, done_one, done_two), shards[3:], SCATTER[3:])
    ]
    totals, gexpand, gproject, gtaps, gmisc, gone, gtwo = backward(
        cells, dcells, project, taps, pre, deep, stats, parts, [s.shape for s in shards], SCATTER, 2
    )
    gfilm, gtable, gsmall = unpack_misc(gmisc)
    grads = (
        jnp.concatenate([gexpand.T, gproject.T, gtaps[:9, :24]], 0),
        jnp.concatenate([gfilm, gtable], 1).T,
        gsmall.T,
        jnp.stack([gone[:, 128 * j : 128 * j + 128] for j in range(4)]),
        jnp.moveaxis(gtwo.reshape(16, 2, 512), 1, 0),
        gone[:, 512 : 512 + DIMS * 64].reshape(16, DIMS, 64),
    )
    loss_sum, count, square = (jnp.sum(totals[8 * i : 8 * i + 8]) for i in range(3))
    loss_sum, count = 0.5 * loss_sum, 0.5 * count
    norm = jnp.sqrt(square) / count
    factor = jnp.minimum(1.0, CLIP_NORM / norm) / count
    steps_done = step_count[0].astype(f32)
    masters = (conv_w, cond_w, small_w, attn_w, mlp_w, head_w)
    firsts = (conv_m1, cond_m1, small_m1, attn_m1, mlp_m1, head_m1)
    seconds = (conv_m2, cond_m2, small_m2, attn_m2, mlp_m2, head_m2)
    outs = [loss_sum / count, norm]
    for idx in range(6):
        outs.extend(adam(masters[idx], firsts[idx], seconds[idx], grads[idx] * factor, steps_done, RATES[idx]))
    return tuple(outs)


def solution(mesh):
    torus = Mesh(mesh.devices.reshape(2, 4, 4, 2, 2), NAMES)
    weights = (
        *[P(None, DP_MP)] * 9,
        *[P(None, DP, MP)] * 6,
        *[P(DP, None, MP)] * 3,
    )
    data = (P(DP_MP, None, None), P(DP_MP), P(DP), P(DP, None), P(DP), P())
    return jax.shard_map(
        per_device, mesh=torus, in_specs=(*data, *weights), out_specs=(P(), P(), *weights), check_vma=False
    )
```

time: 369 us -> 276 us (0.75)
  Pallas kernels: 322 us -> 242 us
  local copies, waits for them, and re-layouts: 19.2 us -> 11.3 us
  waiting for transfers between devices: 5.27 us -> 0 us
    pallas_call x4 -> x2, Pallas kernels: 233 us -> 155 us  [the longest x1 87.4 us: backward(): pl.pallas_call(functools.partial(backward_kernel, plan), out_shape=[shape...]
    ppermute x1 -> x0, waiting for transfers between devices: 5.27 us -> none  [swap_cores(): return lax.ppermute(value, 'mp_1', [(0, 1), (1, 0)])]
  transfers between devices with their start and end apart: 1 -> 0, of which waited for: 1 -> 0; matrix products, arithmetic and copies ran while one was open for 0% -> 0% of each run, Pallas kernels for 0% -> 0%
where the time goes in v1:
time: 276 us; the launch traced here: 272 us
  Pallas kernels  242 us (88%)
  other arithmetic  11.5 us (4%)
  local copies, waits for them, and re-layouts  11.3 us (4%)
  between operations  7.05 us (3%)
    pallas_call x1, Pallas kernels, backward(): pl.pallas_call(functools.partial(backward_kernel, plan), out_shape=[shape...  87.4 us
    pallas_call x1, Pallas kernels, middle(): pl.pallas_call(middle_kernel, out_shape=[jax.ShapeDtypeStruct((PIX * PAIR...  87.1 us
    pallas_call x1, Pallas kernels, forward(): pl.pallas_call(functools.partial(forward_kernel, plan), out_shape=[shape(...  67.5 us

profile of v1, /device:TPU:1, one launch (start us, length us, event | category | flops | bytes accessed | tf_op | source)
XLA Modules:
  0.0 271.8 jit_solution(2420472377359119388)
XLA Ops:
  0.7 0.0 copy-start
  0.7 0.8 convert_bitcast_fusion.1
  1.5 0.7 convert_bitcast_fusion.2
  2.2 0.1 fusion.29
  2.2 0.6 pad_maximum_fusion.1.refs_5_
  2.9 0.8 convert_element_type.47
  3.7 0.9 convert_element_type.48
  4.6 0.1 reshape.101
  4.7 0.6 pad.18.refs_6_
  5.3 1.1 copy.55
  6.4 0.7 copy.58.refs_2_
  7.1 0.7 copy.59.refs_3_
  7.8 0.7 tile.4
  8.5 0.1 tile.10
  8.6 0.7 broadcast_in_dim.14.refs_1_
  9.2 0.6 pad.16.refs_4_
  9.9 0.8 convert_bitcast_fusion
  10.7 0.6 copy.72
  11.3 67.5 %shard_map.383 = (s32[2,24,128]{2,1,0:T(8,128)}, bf16[1944,512]{1,0:T(8,128)(2,1)}, bf16[4,2,4,2,24,512]{5,4,3,2,1,0:T(8,128)(2,1)}, f32[4,16,384]{2,1,0:T(8,128...) custom-call(bf16[12,81,512]{2,1,0:T(8,128)(2,1)} %refs_0_.1, ...), custom_call_target="tpu_custom_call" | custom-call | tf_op jit(solution)/shard_map/pallas_call | solution.py:801
  78.8 0.1 constant_dynamic-slice_fusion
  78.9 0.1 copy.70
  79.0 0.6 pad.19.bins
  79.6 0.1 dynamic-slice_convert_fusion
  79.7 0.7 broadcast_in_dim.32.mask
  80.3 0.1 dynamic_slice.9
  80.4 0.1 broadcast_in_dim.29
  80.5 0.1 broadcast_in_dim.30
  80.6 0.7 broadcast_in_dim.31.instr
  81.2 87.1 %shard_map.384 = (bf16[1944,512]{1,0:T(8,128)(2,1)}, bf16[1024,512]{1,0:T(8,128)(2,1)}, bf16[2,512,1280]{2,1,0:T(8,128)(2,1)}, bf16[2,512,1024]{2,1,0:T(8,128)(2,1)}, f32[16,128]{1,0:T(8,128)}) custom-call(s32[1]{0:T(128)} %bitcast.8.core_ref, f32[1944,512]{1,0:T(8,128)} %get-tuple-element.43.part, bf16[1944,512]{1,0:T(8,128)(2,1)} %get-tuple-element.42.cells.refs_0_, ...), custom_call_target="tpu_custom_call" | custom-call | tf_op jit(solution)/shard_map/pallas_call | solution.py:614
  168.3 0.0 copy-start.9
  168.3 0.0 copy-start.3
  168.4 0.0 copy-start.10
  168.4 0.0 copy-start.11
  168.4 0.0 copy-start.4
  168.4 0.0 copy-start.15
  168.4 0.0 copy-start.16
  168.4 87.4 %shard_map.385 = (f32[24,128]{1,0:T(8,128)}, f32[24,512]{1,0:T(8,128)}, f32[24,512]{1,0:T(8,128)}, f32[16,128]{1,0:T(8,128)}, f32[16,512]{1,0:T(8,128)}, /*index=5*/f32[16,1280]{1,0:T(8,128)}, f32[16,1024]{1,0:T(8,128)}) custom-call(bf16[1944,512]{1,0:T(8,128)(2,1)} %get-tuple-element.42.cells.refs_0_, bf16[1944,512]{1,0:T(8,128)(2,1)} %get-tuple-element.48.refs_1_, ...), custom_call_target="tpu_custom_call" | custom-call | tf_op jit(solution)/shard_map/pallas_call | solution.py:1093
  255.8 0.0 copy-start.20
  255.8 0.0 copy-start.21
  255.9 0.0 copy-start.22
  255.9 0.0 copy-start.5
  255.9 0.0 copy-start.17
  255.9 0.0 copy-start.18
  255.9 0.0 copy-start.19
  255.9 0.0 copy-start.1
  255.9 0.0 copy-start.6
  255.9 0.0 copy-start.7
  256.0 1.4 slice_reduce_fusion
  259.5 0.8 slice_multiply_fusion
  260.3 0.1 mul.369
  261.1 0.2 copy_subtract_fusion
  261.3 0.7 copy.67
  262.0 0.7 copy.68
  262.7 0.7 copy.69
  263.3 0.8 broadcast_multiply_fusion
  264.2 0.0 copy-done.3
  264.2 0.7 multiply_subtract_fusion.1
  264.9 0.7 slice_bitcast_fusion.3
  265.6 0.0 copy-done.15
  265.6 0.7 multiply_subtract_fusion.2
  266.3 0.7 multiply_subtract_fusion.4
  267.0 0.7 multiply_subtract_fusion.3
  267.7 0.1 copy.61
  267.8 0.8 multiply_subtract_fusion
  (41 shorter events, 0.2 us)
Async XLA Ops:
  0.7 78.1 %copy-start = (s32[48,11]{0,1:T(8,128)S(1)}, s32[48,11]{0,1:T(8,128)}, u32[]{:S(2)}) copy-start(s32[48,11]{0,1:T(8,128)} %param.27) | copy-start | bytes 6340
  0.7 78.9 %copy-start.23 = (s32[48]{0:T(128)S(1)}, s32[48]{0:T(128)}, u32[]{:S(2)}) copy-start(s32[48]{0:T(128)} %param.28) | copy-start | bytes 580
  0.7 79.6 %copy-start.24 = (s32[8]{0:T(128)S(1)}, s32[8]{0:T(128)}, u32[]{:S(2)}) copy-start(s32[8]{0:T(128)} %param.26) | copy-start | bytes 100
  168.3 92.8 %copy-start.2 = (f32[16,11,64]{2,0,1:T(8,128)S(1)}, f32[16,11,64]{2,0,1:T(8,128)}, u32[]{:S(2)}) copy-start(f32[16,11,64]{2,0,1:T(8,128)} %param.45) | copy-start | bytes 135172
  168.3 92.8 %copy-start.8 = (f32[16,11,64]{2,0,1:T(8,128)S(1)}, f32[16,11,64]{2,0,1:T(8,128)}, u32[]{:S(2)}) copy-start(f32[16,11,64]{2,0,1:T(8,128)} %param.47) | copy-start | bytes 135172
  168.3 92.8 %copy-start.9 = (f32[16,11,64]{2,0,1:T(8,128)S(1)}, f32[16,11,64]{2,0,1:T(8,128)}, u32[]{:S(2)}) copy-start(f32[16,11,64]{2,0,1:T(8,128)} %param.46) | copy-start | bytes 135172
  168.3 95.8 %copy-start.3 = (f32[2,16,512]{2,1,0:T(8,128)S(1)}, f32[2,16,512]{2,1,0:T(8,128)}, u32[]{:S(2)}) copy-start(f32[2,16,512]{2,1,0:T(8,128)} %param.42) | copy-start | bytes 196612
  168.4 95.8 %copy-start.10 = (f32[2,16,512]{2,1,0:T(8,128)S(1)}, f32[2,16,512]{2,1,0:T(8,128)}, u32[]{:S(2)}) copy-start(f32[2,16,512]{2,1,0:T(8,128)} %param.44) | copy-start | bytes 196612
  168.4 95.8 %copy-start.11 = (f32[2,16,512]{2,1,0:T(8,128)S(1)}, f32[2,16,512]{2,1,0:T(8,128)}, u32[]{:S(2)}) copy-start(f32[2,16,512]{2,1,0:T(8,128)} %param.43) | copy-start | bytes 196612
  168.4 97.2 %copy-start.4 = (f32[4,16,128]{2,1,0:T(8,128)S(1)}, f32[4,16,128]{2,1,0:T(8,128)}, u32[]{:S(2)}) copy-start(f32[4,16,128]{2,1,0:T(8,128)} %param.39) | copy-start | bytes 98308
  168.4 97.2 %copy-start.15 = (f32[4,16,128]{2,1,0:T(8,128)S(1)}, f32[4,16,128]{2,1,0:T(8,128)}, u32[]{:S(2)}) copy-start(f32[4,16,128]{2,1,0:T(8,128)} %param.41) | copy-start | bytes 98308
  168.4 97.2 %copy-start.16 = (f32[4,16,128]{2,1,0:T(8,128)S(1)}, f32[4,16,128]{2,1,0:T(8,128)}, u32[]{:S(2)}) copy-start(f32[4,16,128]{2,1,0:T(8,128)} %param.40) | copy-start | bytes 98308
  255.8 10.5 %copy-start.14 = (f32[16,512]{1,0:T(8,128)S(1)}, f32[16,512]{1,0:T(8,128)}, u32[]{:S(2)}) copy-start(f32[16,512]{1,0:T(8,128)} %get-tuple-element.61) | copy-start | bytes 98308
  255.8 10.5 %copy-start.20 = (f32[11,4]{0,1:T(4,128)S(1)}, f32[11,4]{0,1:T(4,128)}, u32[]{:S(2)}) copy-start(f32[11,4]{0,1:T(4,128)} %param.36) | copy-start | bytes 532
  255.8 10.5 %copy-start.21 = (f32[11,4]{0,1:T(4,128)S(1)}, f32[11,4]{0,1:T(4,128)}, u32[]{:S(2)}) copy-start(f32[11,4]{0,1:T(4,128)} %param.38) | copy-start | bytes 532
  255.9 10.5 %copy-start.22 = (f32[11,4]{0,1:T(4,128)S(1)}, f32[11,4]{0,1:T(4,128)}, u32[]{:S(2)}) copy-start(f32[11,4]{0,1:T(4,128)} %param.37) | copy-start | bytes 532
  255.9 11.1 %copy-start.5 = (f32[1770,4]{0,1:T(4,128)S(1)}, f32[1770,4]{0,1:T(4,128)}, u32[]{:S(2)}) copy-start(f32[1770,4]{0,1:T(4,128)} %param.33) | copy-start | bytes 84964
  255.9 11.1 %copy-start.17 = (f32[1770,4]{0,1:T(4,128)S(1)}, f32[1770,4]{0,1:T(4,128)}, u32[]{:S(2)}) copy-start(f32[1770,4]{0,1:T(4,128)} %param.35) | copy-start | bytes 84964
  255.9 11.1 %copy-start.18 = (f32[1770,4]{0,1:T(4,128)S(1)}, f32[1770,4]{0,1:T(4,128)}, u32[]{:S(2)}) copy-start(f32[1770,4]{0,1:T(4,128)} %param.34) | copy-start | bytes 84964
  255.9 11.8 %copy-start.19 = (f32[16,128]{1,0:T(8,128)S(1)}, f32[16,128]{1,0:T(8,128)}, u32[]{:S(2)}) copy-start(f32[16,128]{1,0:T(8,128)} %get-tuple-element.60) | copy-start | bytes 24580
  255.9 11.9 %copy-start.1 = (f32[1033,24]{0,1:T(8,128)S(1)}, f32[1033,24]{0,1:T(8,128)}, u32[]{:S(2)}) copy-start(f32[1033,24]{0,1:T(8,128)} %param.30) | copy-start | bytes 297508
  255.9 11.9 %copy-start.6 = (f32[1033,24]{0,1:T(8,128)S(1)}, f32[1033,24]{0,1:T(8,128)}, u32[]{:S(2)}) copy-start(f32[1033,24]{0,1:T(8,128)} %param.32) | copy-start | bytes 297508
  255.9 11.9 %copy-start.7 = (f32[1033,24]{0,1:T(8,128)S(1)}, f32[1033,24]{0,1:T(8,128)}, u32[]{:S(2)}) copy-start(f32[1033,24]{0,1:T(8,128)} %param.31) | copy-start | bytes 297508
  256.0 11.9 %copy-start.12 = (f32[24,512]{1,0:T(8,128)S(1)}, f32[24,512]{1,0:T(8,128)}, u32[]{:S(2)}) copy-start(f32[24,512]{1,0:T(8,128)} %get-tuple-element.58) | copy-start | bytes 147460
  256.0 11.9 %copy-start.13 = (f32[24,512]{1,0:T(8,128)S(1)}, f32[24,512]{1,0:T(8,128)}, u32[]{:S(2)}) copy-start(f32[24,512]{1,0:T(8,128)} %get-tuple-element.59) | copy-start | bytes 147460

commit v2 on v1

--- a/solution.py
+++ b/solution.py
@@ -69,13 +69,26 @@
     return tuple(SIZES[d] for d in dims)
 
 
-def greet(me):
+def announce(me, wide=False):
     barrier = pltpu.get_barrier_semaphore()
-    for axis in "xyz":
-        for k in range(1, RING):
-            pl.semaphore_signal(barrier, inc=1, device_id=device_of(axis, ring(me[axis], k)), device_id_type=MESH_ID)
-    pl.semaphore_signal(barrier, inc=1, device_id=device_of("c", 1 - me["c"]), device_id_type=MESH_ID)
-    pl.semaphore_wait(barrier, 10)
+    peers = [{a: k} for a in "xyz" for k in range(1, RING)] + [{"c": 1}]
+    if wide:
+        peers += [{"x": k, "c": 1} for k in range(1, RING)]
+        peers += [{"y": j, "z": k} for j in range(1, RING) for k in range(1, RING)]
+    for moves in peers:
+        pl.semaphore_signal(barrier, inc=1, device_id=moved(me, moves), device_id_type=MESH_ID)
+    return len(peers)
+
+
+def moved(me, moves):
+    found = {}
+    for axis, k in moves.items():
+        found.update(device_of(axis, lax.rem(me[axis] + k, 2 if axis == "c" else RING)))
+    return found
+
+
+def meet(count):
+    pl.semaphore_wait(pltpu.get_barrier_semaphore(), count)
 
 
 def remote(src, dst, send, recv, axis, at):
@@ -257,11 +270,11 @@
 OWNED = ("x", "l", "z", "h")
 GATHER = (
     (OWNED, ("z", "y", "x")),
-    (OWNED, ("y", "z", "x")),
+    (OWNED, ("x", "z", "y")),
     (OWNED, ("z", "y", "x")),
-    (("c", "l", "z", "x", "h"), ("x", "y", "z")),
-    (("h", "c", "l", "z", "x"), ("x", "z", "y")),
-    (("h", "c", "l", "z", "x"), ("x", "y", "z")),
+    (("c", "l", "z", "x", "h"), ("z", "x", "y")),
+    (("h", "c", "l", "z", "x"), ("y", "x", "z")),
+    (("h", "c", "l", "z", "x"), ("z", "y", "x")),
 )
 SCATTER = (
     (OWNED, ("z", "y", "x")),
@@ -271,6 +284,7 @@
     (("h", "l", "z", "x"), ("x", "y", "z")),
     (("h", "l", "z", "x"), ("y", "x", "z")),
 )
+SLABS = ((24, 512), (24, 512), (16, 128), (16, 512), (16, 1280), (16, 1024))
 
 
 D, EXP, MAP, PIX = 512, 3072, 9, 81
@@ -319,6 +333,7 @@
 INSTR, DIMS, BINS, NTOK, FRAMES, HEADS, HD = 744, 11, 256, 8, 6, 8, 64
 TABLE = INSTR + 2
 ROWS = PAIR * NTOK
+PADDED = 2048
 SMALL_AT = TABLE - D
 LN_EPS = 1e-06
 OUT_MULT = 2.0
@@ -373,12 +388,24 @@
     return (iota((rows, D), 0) + start == row).astype(bf16)
 
 
+def over_cells(body, carry):
+    many = 16 * PAIR
+    carry = lax.fori_loop(
+        0, PIX // 16, lambda i, c: body(pl.ds(pl.multiple_of(i * many, many), many), many, c), carry
+    )
+    return body(slice(PIX // 16 * many, PIX * PAIR), PAIR, carry)
+
+
 def middle_kernel(
-    core_ref, part, cells, misc, one, two, instr, cam, bins, mask,
-    dcells, dmisc, done_one, done_two, stats,
-    y, logit, att, qkv, prob, ctx, up, hid, acc, dlog, lowgrad,
+    core_ref, part, cells, misc, one_in, two_in, instr, cam, bins, mask,
+    dcells, dmisc, one_out, two_out, stats,
+    one, two, done_one, done_two, y_hi, y_lo, logit, att, qkv, prob, ctx, up, hid, acc, dlog, lowgrad, sems,
 ):
     core = core_ref[0]
+    fetch_one = pltpu.make_async_copy(one_in, one, sems.at[0])
+    fetch_two = pltpu.make_async_copy(two_in, two, sems.at[1])
+    fetch_one.start()
+    fetch_two.start()
     lanes = iota((PAIR, 128), 1)
 
     def chosen(tile):
@@ -397,41 +424,54 @@
     pick = (iota((16, D), 1) == SMALL_AT + iota((16, D), 0)).astype(bf16)
     small = nn(nt(pick, flat).astype(bf16), place_of_feature(0, 2048))
     gains = [small[i : i + 1] for i in range(3)]
-    learner = jnp.concatenate([small[3:11], jnp.zeros((120, D), f32)], axis=0)
-
-    def feature(cell, _):
-        rows = pl.ds(pl.multiple_of(cell * PAIR, PAIR), PAIR)
-        v = cells[rows, :].astype(f32) + part[rows, :] * scale + beta
-        y[rows, :] = v
+    learner = jnp.concatenate([small[3:11], jnp.zeros((120, D), f32)], axis=0).astype(bf16)
+
+    def feature(rows, size, _):
+        v = part[rows, :].reshape(size // PAIR, PAIR, D) * scale + beta
+        v = v.reshape(size, D) + cells[rows, :].astype(f32)
+        hi = v.astype(bf16)
+        y_hi[rows, :] = hi
+        y_lo[rows, :] = (v - hi.astype(f32)).astype(bf16)
         return 0
 
-    lax.fori_loop(0, PIX, feature, 0)
-    logit[...] = (
-        lax.dot_general(y[...], learner, (((1,), (1,)), ((), ())), precision=HIGH, preferred_element_type=f32) * LEARN
-    )
+    over_cells(feature, 0)
+    tail = slice(PIX * PAIR, PADDED)
+    for ref in (y_hi, y_lo, att, logit):
+        ref[tail, :] = jnp.zeros((PADDED - PIX * PAIR, ref.shape[1]), ref.dtype)
+    used = slice(0, PIX * PAIR)
+    logit[used, :] = (nt(y_hi[used, :], learner) + nt(y_lo[used, :], learner)) * LEARN
 
     def softmax_over_cells(v):
         v = v.reshape(PIX, PAIR, 128)
         e = jnp.exp(v - jnp.max(v, 0, keepdims=True))
         return e / jnp.sum(e, 0, keepdims=True)
 
-    att[...] = softmax_over_cells(logit[...]).reshape(PIX * PAIR, 128)
+    att[used, :] = softmax_over_cells(logit[used, :]).reshape(PIX * PAIR, 128)
     acc[...] = jnp.zeros_like(acc)
-    for half in range(2):
-        columns = slice(256 * half, 256 * half + 256)
-
-        zero = jnp.zeros((PAIR, 256), f32)
-        for t0 in range(0, NTOK, 4):
-
-            def gather_some(cell, totals, t0=t0, columns=columns):
-                rows = pl.ds(pl.multiple_of(cell * PAIR, PAIR), PAIR)
-                a, v = att[rows, :], y[rows, columns]
-                return tuple(t + a[:, t0 + i : t0 + i + 1] * v for i, t in enumerate(totals))
-
-            totals = lax.fori_loop(0, PIX, gather_some, (zero,) * 4)
-            for i in range(4):
-                acc[(t0 + i) * PAIR : (t0 + i + 1) * PAIR, columns] = totals[i]
+
+    def gather(i, _):
+        rows = pl.ds(pl.multiple_of(i * 512, 512), 512)
+        turned = jnp.concatenate(
+            [att[pl.ds(pl.multiple_of(i * 512 + 128 * k, 128), 128), :].T[0:NTOK] for k in range(4)], axis=1
+        )
+        hi = turned.astype(bf16).astype(f32)
+        lo = turned - hi
+        image = lax.rem(i * 512 + iota((8, 512), 1), PAIR)
+        own = [image == 8 * g + iota((8, 512), 0) for g in range(3)]
+
+        def wide(v):
+            pieces = [jnp.where(m, v[t : t + 1], 0.0) for t in range(NTOK) for m in own]
+            return jnp.concatenate(pieces, axis=0).astype(bf16)
+
+        wide_hi = wide(hi)
+        upper = y_hi[rows, :]
+        acc[...] += nn(wide_hi, upper) + nn(wide(lo), upper) + nn(wide_hi, y_lo[rows, :])
+        return 0
+
+    lax.fori_loop(0, PADDED // 512, gather, 0)
     tok = acc[...].astype(bf16).astype(f32)
+    fetch_one.wait()
+    fetch_two.wait()
 
     h1, normed1, inverse1 = norm_fwd(tok, gains[0])
     h1_low = h1.astype(bf16)
@@ -565,38 +605,56 @@
     dtok_norm, dgain0 = norm_back(normed1, inverse1, gains[0], acc[...])
     acc[...] = dx1 + dtok_norm
 
-    def slope_of(cell, _):
-        rows = pl.ds(pl.multiple_of(cell * PAIR, PAIR), PAIR)
-        v = y[rows, :]
-        found = jnp.zeros((PAIR, 128), f32)
-        for t in range(NTOK):
-            s = jnp.sum(v * acc[t * PAIR : (t + 1) * PAIR, :], -1, keepdims=True)
-            found = jnp.where(lanes == t, s, found)
-        logit[rows, :] = found
+    send_one = pltpu.make_async_copy(done_one, one_out, sems.at[0])
+    send_two = pltpu.make_async_copy(done_two, two_out, sems.at[1])
+    send_one.start()
+    send_two.start()
+    dtok_hi = acc[...].astype(bf16)
+    dtok_lo = (acc[...] - dtok_hi.astype(f32)).astype(bf16)
+    same = lax.rem(iota((PAIR, ROWS), 1), PAIR) == iota((PAIR, ROWS), 0)
+    token_of = (lax.div(iota((128, ROWS), 1), PAIR) == iota((128, ROWS), 0)).astype(bf16)
+
+    def own_image(v):
+        return jnp.where(same, v.reshape(-1, PAIR, ROWS), 0.0).reshape(-1, ROWS)
+
+    def halves(v):
+        hi = v.astype(bf16)
+        return hi, (v - hi.astype(f32)).astype(bf16)
+
+    def slope_of(rows, size, _):
+        upper = y_hi[rows, :]
+        g = own_image(nt(upper, dtok_hi) + nt(upper, dtok_lo) + nt(y_lo[rows, :], dtok_hi))
+        hi, lo = halves(g)
+        logit[rows, :] = nt(hi, token_of) + nt(lo, token_of)
         return 0
 
-    lax.fori_loop(0, PIX, slope_of, 0)
-    a = att[...].reshape(PIX, PAIR, 128)
-    da = logit[...].reshape(PIX, PAIR, 128)
-    logit[...] = (a * (da - jnp.sum(a * da, 0, keepdims=True)) * LEARN).reshape(PIX * PAIR, 128)
-    dlearner = lax.dot_general(logit[...], y[...], (((0,), (0,)), ((), ())), precision=HIGH, preferred_element_type=f32)
-
-    def spread(cell, sums):
-        rows = pl.ds(pl.multiple_of(cell * PAIR, PAIR), PAIR)
-        a, dl = att[rows, :], logit[rows, :]
-        dy = jnp.zeros((PAIR, D), f32)
-        for t in range(NTOK):
-            dy = dy + a[:, t : t + 1] * acc[t * PAIR : (t + 1) * PAIR, :] + dl[:, t : t + 1] * learner[t : t + 1]
-        dcells[rows, :] = (dy * scale).astype(bf16)
-        return sums[0] + dy * part[rows, :], sums[1] + dy
+    over_cells(slope_of, 0)
+    a = att[used, :].reshape(PIX, PAIR, 128)
+    da = logit[used, :].reshape(PIX, PAIR, 128)
+    logit[used, :] = (a * (da - jnp.sum(a * da, 0, keepdims=True)) * LEARN).reshape(PIX * PAIR, 128)
+    turned = jnp.concatenate([logit[128 * k : 128 * k + 128, :].T[0:NTOK] for k in range(PADDED // 128)], axis=1)
+    upper = turned.astype(bf16).astype(f32)
+    both = jnp.concatenate([upper, turned - upper], axis=0).astype(bf16)
+    sums = nn(both, y_hi[...])
+    dlearner = sums[0:8] + sums[8:16] + nn(both, y_lo[...])[0:8]
+
+    def spread(rows, size, sums):
+        hi, lo = halves(att[rows, :])
+        hi, lo = own_image(nn(hi, token_of)).astype(bf16), own_image(nn(lo, token_of)).astype(bf16)
+        slope_hi, slope_lo = halves(logit[rows, :])
+        dy = nn(hi, dtok_hi) + nn(lo, dtok_hi) + nn(hi, dtok_lo) + nn(slope_hi, learner) + nn(slope_lo, learner)
+        dy = dy.reshape(size // PAIR, PAIR, D)
+        dcells[rows, :] = (dy * scale).astype(bf16).reshape(size, D)
+        p = part[rows, :].reshape(size // PAIR, PAIR, D)
+        return sums[0] + jnp.sum(dy * p, 0), sums[1] + jnp.sum(dy, 0)
 
     zero = jnp.zeros((PAIR, D), f32)
-    dgamma, dbeta = lax.fori_loop(0, PIX, spread, (zero, zero))
+    dgamma, dbeta = over_cells(spread, (zero, zero))
     dgamma, dbeta = dgamma.astype(bf16), dbeta.astype(bf16)
     dcvec = only(nt(dgamma, flat) + shifted(nt(dbeta, flat), 4), 0) * FILM
     high = dcvec.astype(bf16).astype(f32)
     rest = dcvec - high
-    dsmall = jnp.concatenate([dgain0, dgain1, dgain2, dlearner[0:8], jnp.zeros((5, D), f32)], axis=0).astype(bf16)
+    dsmall = jnp.concatenate([dgain0, dgain1, dgain2, dlearner, jnp.zeros((5, D), f32)], axis=0).astype(bf16)
     mine = pl.ds(pl.multiple_of(core * 1024, 1024), 1024)
     lhs = jnp.concatenate(
         [cvec, cvec_4, shifted(high, 120), shifted(rest, 120), shifted(high, 116), shifted(rest, 116)], axis=0
@@ -607,6 +665,8 @@
     result = tn(lhs, rhs)
     film_rows = (iota((1024, D), 0) & 15) < 8
     dmisc[...] = jnp.where(film_rows, result * FILM, result).astype(bf16)
+    send_one.wait()
+    send_two.wait()
 
 
 def middle(core, part, cells, misc, one, two, instr, cam, bins, mask):
@@ -620,12 +680,17 @@
             jax.ShapeDtypeStruct((2, D, 1024), bf16),
             jax.ShapeDtypeStruct((16, 128), f32),
         ],
-        in_specs=[pl.BlockSpec(memory_space=pltpu.SMEM)] + [vmem] * 9,
-        out_specs=[vmem] * 5,
+        in_specs=[pl.BlockSpec(memory_space=pltpu.SMEM)] + [vmem] * 3 + [ANY] * 2 + [vmem] * 4,
+        out_specs=[vmem, vmem, ANY, ANY, vmem],
         scratch_shapes=[
-            pltpu.VMEM((PIX * PAIR, D), f32),
-            pltpu.VMEM((PIX * PAIR, 128), f32),
-            pltpu.VMEM((PIX * PAIR, 128), f32),
+            pltpu.VMEM((4, D, 1280), bf16),
+            pltpu.VMEM((4, D, 1024), bf16),
+            pltpu.VMEM((2, D, 1280), bf16),
+            pltpu.VMEM((2, D, 1024), bf16),
+            pltpu.VMEM((PADDED, D), bf16),
+            pltpu.VMEM((PADDED, D), bf16),
+            pltpu.VMEM((PADDED, 128), f32),
+            pltpu.VMEM((PADDED, 128), f32),
             pltpu.VMEM((4, ROWS, 384), bf16),
             pltpu.VMEM((4, 2, ROWS, ROWS), f32),
             pltpu.VMEM((4, ROWS, 128), bf16),
@@ -634,6 +699,7 @@
             pltpu.VMEM((ROWS, D), f32),
             pltpu.VMEM((4, PAIR, 768), bf16),
             pltpu.VMEM((4, ROWS, 512), bf16),
+            pltpu.SemaphoreType.DMA((2,)),
         ],
         compiler_params=pltpu.CompilerParams(vmem_limit_bytes=VMEM_BYTES),
     )(core, part, cells, misc, one, two, instr, cam, bins, mask)
@@ -657,26 +723,59 @@
         cells[first * PAIR : first * PAIR + rows, :] = nn(turn, block).astype(bf16)
 
 
+def fill_shards(conv, cond, small, attn, mlp, head, camera, core, shards, staged, tap_tile, cam):
+    shards[0][...] = conv[:, 0:D].astype(bf16)
+    shards[1][...] = conv[:, D : 2 * D].astype(bf16)
+    tap_tile[...] = jnp.zeros_like(tap_tile)
+    tap_tile[0:24, 0:9] = conv[:, 2 * D :]
+    shards[2][...] = tap_tile[...].T[0:16].astype(bf16)
+    staged[...] = jnp.zeros_like(staged)
+    for i in range(3):
+        staged[4 * i : 4 * i + 4, :] = cond[:, D * i : D * i + D]
+    staged[12:16, 0:SMALL_AT] = cond[:, 3 * D :]
+    staged[12:16, SMALL_AT : SMALL_AT + 11] = small[...]
+    shards[3][...] = staged[...].astype(bf16)
+    for j in range(4):
+        shards[4][:, 128 * j : 128 * j + 128] = attn[j].astype(bf16)
+    for k in range(0, DIMS - 1, 2):
+        both = jnp.concatenate([head[k], head[k + 1]], axis=1)
+        shards[4][:, 512 + 64 * k : 640 + 64 * k] = both.astype(bf16)
+    last = jnp.concatenate([head[DIMS - 1], jnp.zeros((16, 64), f32)], axis=1)
+    shards[4][:, 1152:1280] = last.astype(bf16)
+    for j in range(2):
+        shards[5][:, 512 * j : 512 * j + 512] = mlp[j].astype(bf16)
+    row = iota((PAIR, 128), 0)
+    found = jnp.zeros((PAIR, 128), jnp.int32)
+    for i in range(PAIR // 2):
+        found = jnp.where(row == core * (PAIR // 2) + i, camera[i], found)
+    cam[...] = found
+
+
 def forward_kernel(plan, *refs):
     n = len(plan)
-    pairs, shards = refs[0:2], refs[2 : 2 + n]
+    frames, camera = refs[0:2]
+    masters = refs[2 : 2 + n]
     refs = refs[2 + n :]
     cam2, cells_out, project_out, taps_out, misc_out, one_out, two_out, pre_out, deep_out, total_out = refs[:10]
     frames2, cells, expand, project, slabs, taps, places, act, pre, deep, part, other = refs[10:22]
-    send, recv, fsend, frecv, local, kept, swap_send, swap_recv = refs[22:]
+    shards, staged, tap_tile, cam = refs[22 : 22 + n], refs[22 + n], refs[23 + n], refs[24 + n]
+    send, recv, fsend, frecv, local, kept, swap_send, swap_recv = refs[25 + n :]
     me = here()
-    greet(me)
+    count = announce(me)
+    fill_shards(*masters, camera, me["c"], shards, staged, tap_tile, cam)
+    meet(count)
     swaps = []
-    for i, out in enumerate((frames2, cam2)):
-        mine = pltpu.make_async_copy(pairs[i], out.at[me["c"]], local.at[n + i])
+    for i, (src, out) in enumerate(((frames, frames2), (cam, cam2))):
+        mine = pltpu.make_async_copy(src, out.at[me["c"]], local.at[n + i])
         mine.start()
-        swaps += [mine, remote(pairs[i], out.at[me["c"]], swap_send.at[i], swap_recv.at[i], "c", 1 - me["c"])]
+        swaps += [mine, remote(src, out.at[me["c"]], swap_send.at[i], swap_recv.at[i], "c", 1 - me["c"])]
     outs = (expand, project, slabs, misc_out, one_out, two_out)
     jobs = [
         Gather(me, dims, order, shards[b], outs[b], send.at[b], recv.at[b], fsend.at[b], frecv.at[b], local.at[b])
         for b, (dims, order) in enumerate(plan)
     ]
-    first, rest = jobs[:3], jobs[3:]
+    early, late, rest = (jobs[0], jobs[2]), (jobs[1],), jobs[3:]
+    first = jobs[:3]
 
     def relay(some, phase):
         for job in some:
@@ -688,18 +787,18 @@
 
     for job in jobs:
         job.begin()
-    clear_borders(act)
-    part[...] = jnp.zeros_like(part)
-    places[...] = tap_places()
     relay(first, 0)
     finish(first, 0)
-    swaps[0].wait()
-    swaps[1].wait()
-    to_cells(frames2, cells)
+    clear_borders(act)
+    places[...] = tap_places()
     relay(first, 1)
     finish(first, 1)
     relay(rest, 0)
     finish(rest, 0)
+    part[...] = jnp.zeros_like(part)
+    swaps[0].wait()
+    swaps[1].wait()
+    to_cells(frames2, cells)
     saves = []
 
     def save(src, dst, number):
@@ -708,20 +807,19 @@
         saves.append(copy)
 
     save(cells, cells_out, 0)
-    spans = [None] * STEPS
+    spans, leaves = [None] * STEPS, []
     for step in range(STEPS):
         slot = step % 2
         at = ring(me["x"], (0, -1, 1, 2)[step])
         if step == 1:
-            relay(first, 2)
+            relay(early, 2)
+            relay(late, 2)
         if step == 3:
-            finish(first, 2)
-            save(project, project_out, 1)
+            finish(early, 2)
         if step >= 2:
             for copy in spans[step - 2]:
                 copy.wait()
         weight = expand[at].reshape(WIDTH, D)
-        back = project[at].reshape(WIDTH, D)
         tap = slabs[at].reshape(OWNERS, 16, 128)
         side = jnp.concatenate([tap[i] for i in range(OWNERS)], axis=1)
         taps[at] = nn(side, places[...]) * (8.0 / 3.0)
@@ -762,13 +860,19 @@
         if step == 3:
             finish(rest, 2)
 
-        def leave(i, _, back=back, slot=slot):
+        def leave(i, _, at=at, slot=slot):
+            back = project[at].reshape(WIDTH, D)
             rows = pl.ds(pl.multiple_of(i * SPAN, SPAN), SPAN)
             v = deep[slot, pl.ds(i * CHUNK * MAP, CHUNK * MAP)].reshape(SPAN, WIDTH)
             part[rows, :] += nn((v * sigmoid(v)).astype(bf16), back) * PROJECT
             return 0
 
-        if step < STEPS - 1:
+        leaves.append(leave)
+        if step == 1:
+            finish(late, 2)
+            save(project, project_out, 1)
+            lax.fori_loop(0, MAP // CHUNK, leaves[0], 0)
+        if 0 < step < STEPS - 1:
             lax.fori_loop(0, MAP // CHUNK, leave, 0)
     save(taps, taps_out, 2)
     trades = []
@@ -791,17 +895,16 @@
         copy.wait()
 
 
-def forward(pairs, shards, plan, collective_id):
+def forward(frames, camera, masters, plan, collective_id):
     n = len(plan)
-    frames, cam = pairs
     maps = jax.ShapeDtypeStruct((STEPS, *BLOCK), f32)
     shape = jax.ShapeDtypeStruct
-    full = [shape((*lead(dims), *s.shape), s.dtype) for s, (dims, _) in zip(shards, plan)]
+    full = [shape((*lead(dims), *slab), bf16) for slab, (dims, _) in zip(SLABS, plan)]
     rows = PIX * PAIR
     return pl.pallas_call(
         functools.partial(forward_kernel, plan),
         out_shape=[
-            shape((2, *cam.shape), cam.dtype),
+            shape((2, PAIR, 128), jnp.int32),
             shape((rows, D), bf16),
             full[1],
             shape((STEPS, 16, WIDTH), f32),
@@ -810,7 +913,7 @@
             maps,
             shape((rows, D), f32),
         ],
-        in_specs=[ANY] * (2 + n),
+        in_specs=[ANY, pl.BlockSpec(memory_space=pltpu.SMEM)] + [INVMEM] * n,
         out_specs=[ANY] * 10,
         scratch_shapes=[
             pltpu.VMEM((2, *frames.shape), bf16),
@@ -825,6 +928,10 @@
             pltpu.VMEM((2, *BLOCK), f32),
             pltpu.VMEM((rows, D), f32),
             pltpu.VMEM((rows, D), f32),
+            *[pltpu.VMEM(slab, bf16) for slab in SLABS],
+            pltpu.VMEM((16, D), f32),
+            pltpu.VMEM((128, 128), f32),
+            pltpu.VMEM((PAIR, 128), jnp.int32),
             pltpu.SemaphoreType.DMA((n, 3, 4)),
             pltpu.SemaphoreType.DMA((n, 3, 4)),
             pltpu.SemaphoreType.DMA((n, 7)),
@@ -837,7 +944,7 @@
         compiler_params=pltpu.CompilerParams(
             collective_id=collective_id, has_side_effects=True, vmem_limit_bytes=VMEM_BYTES
         ),
-    )(*pairs, *shards)
+    )(frames, camera, *masters)
 
 
 class Blocks:
@@ -949,7 +1056,7 @@
         return pair
 
     maps = [fetch(0), fetch(1), None, None]
-    greet(me)
+    meet(announce(me, wide=True))
     rest = []
     for b, (dims, order) in enumerate(plan[3:]):
         own = rest_room[13 * b : 13 * b + 13]
@@ -1000,9 +1107,10 @@
                 job.finish(step - 2)
         if step == 2:
             for job in rest:
-                job.relay(1)
+                job.finish(0)
         if step == 3:
-            square = close_rest(square)
+            for job in rest:
+                job.finish(1)
         acc[...] = jnp.zeros_like(acc)
 
         def mix(row, subs, cols, slot=slot, at=at):
@@ -1032,12 +1140,9 @@
         if step == 0:
             for job in rest:
                 job.relay(0)
-        if step == 1:
-            for job in rest:
-                job.finish(0)
         if step == 2:
             for job in rest:
-                job.finish(1)
+                job.relay(1)
         if step > 0:
             for job in first:
                 job.middle(step - 1)
@@ -1052,33 +1157,38 @@
         for job in first:
             job.launch(step)
     for job in first:
+        job.finish(STEPS - 2)
+    square = close_rest(square)
+    for job in first:
         job.relay(STEPS - 1)
-    for job in first:
-        job.finish(STEPS - 2)
     for job in first:
         job.middle(STEPS - 1)
     for b, job in enumerate(first):
         total = job.close(job.finish(STEPS - 1))
         outs[b][...] = total
         square = square + folded(total * total)
-    tile[0, 0:16, :] = stats[...]
-    tile[0, 16:24, :] = square
-    for phase, axis in enumerate("cxyz"):
-        size = 2 if axis == "c" else RING
-        copies = [
-            remote(
-                tile.at[phase], tile_box.at[phase, k - 1], tsend.at[phase, k - 1], trecv.at[phase, k - 1],
-                axis, lax.rem(me[axis] + k, size),
+    lines = [jnp.sum(v, 0, keepdims=True) for v in (stats[0:8], stats[8:16], square)]
+    tile[0] = jnp.concatenate([*lines, jnp.zeros((5, 128), f32)], axis=0)
+    number = 0
+    for phase, (one, two) in enumerate((("c", "x"), ("y", "z"))):
+        spans = [range(2 if a == "c" else RING) for a in (one, two)]
+        moves = [{a: k for a, k in ((one, j), (two, k)) if k} for j in spans[0] for k in spans[1] if j or k]
+        copies = []
+        for move in moves:
+            copy = pltpu.make_async_remote_copy(
+                src_ref=tile.at[phase], dst_ref=tile_box.at[number], send_sem=tsend.at[number],
+                recv_sem=trecv.at[number], device_id=moved(me, move), device_id_type=MESH_ID,
             )
-            for k in range(1, size)
-        ]
+            copy.start()
+            copies.append(copy)
+            number += 1
         for copy in copies:
             copy.wait()
         total = tile[phase]
-        for k in range(size - 1):
-            total = total + tile_box[phase, k]
+        for i in range(number - len(copies), number):
+            total = total + tile_box[i]
         tile[phase + 1] = total
-    stats_out[...] = tile[4]
+    stats_out[...] = tile[2]
 
 
 def backward(cells, dcells, project, taps, pre, deep, stats, parts, slabs, plan, collective_id):
@@ -1092,7 +1202,7 @@
         room += Scatter.scratch(dims, order, slab, bf16)
     return pl.pallas_call(
         functools.partial(backward_kernel, plan),
-        out_shape=[shape((24, 128), f32)] + [shape(s, f32) for s in slabs],
+        out_shape=[shape((8, 128), f32)] + [shape(s, f32) for s in slabs],
         in_specs=[ANY] * 6 + [INVMEM] + [ANY] * (n - 3),
         out_specs=[INVMEM] * (1 + n),
         scratch_shapes=[
@@ -1108,16 +1218,16 @@
             pltpu.VMEM(BLOCK, f32),
             pltpu.VMEM((9, 8, WIDTH), f32),
             *room,
-            pltpu.VMEM((5, 24, 128), f32),
-            pltpu.VMEM((4, 3, 24, 128), f32),
+            pltpu.VMEM((3, 8, 128), f32),
+            pltpu.VMEM((22, 8, 128), f32),
             pltpu.SemaphoreType.DMA((3, STEPS, 8)),
             pltpu.SemaphoreType.DMA((3, STEPS, 8)),
             pltpu.SemaphoreType.DMA((n - 3, 3, 4)),
             pltpu.SemaphoreType.DMA((n - 3, 3, 4)),
             pltpu.SemaphoreType.DMA((n - 3,)),
             pltpu.SemaphoreType.DMA((4 + 2 * STEPS,)),
-            pltpu.SemaphoreType.DMA((4, 3)),
-            pltpu.SemaphoreType.DMA((4, 3)),
+            pltpu.SemaphoreType.DMA((22,)),
+            pltpu.SemaphoreType.DMA((22,)),
         ],
         compiler_params=pltpu.CompilerParams(
             collective_id=collective_id, has_side_effects=True, vmem_limit_bytes=VMEM_BYTES
@@ -1125,11 +1235,10 @@
     )(cells, dcells, project, taps, pre, deep, stats, *parts)
 
 
-TAIL = TABLE + 11
 IMAGES = 12
-MP = ("mp_0", "mp_1")
 DP_MP = NAMES
 DP = ("dp_0", "dp_1", "dp_2")
+MP = ("mp_0", "mp_1")
 CLIP_NORM = 0.02
 BETA_ONE = 0.9
 BETA_TWO = 0.999
@@ -1138,30 +1247,60 @@
 RATES = (0.1, 0.1, 0.2, 0.05, 0.05, 0.2)
 
 
-def adam(master, first, second, grad, t, rate):
-    first_new = BETA_ONE * first + (1.0 - BETA_ONE) * grad
-    second_new = BETA_TWO * second + (1.0 - BETA_TWO) * grad * grad
-    m_hat = first_new / (1.0 - BETA_ONE**t)
-    v_hat = second_new / (1.0 - BETA_TWO**t)
-    master_new = master - rate * (m_hat / (jnp.sqrt(v_hat) + ADAM_EPS) + DECAY * master)
-    return [master_new, first_new, second_new]
-
-
-def pack_misc(film, table, small):
-    tail = jnp.concatenate([table, small], axis=1)
-    tail = jnp.pad(tail, ((0, 0), (0, 2 * D - tail.shape[1])))
-    return jnp.concatenate([film[:, :D], film[:, D:], tail[:, :D], tail[:, D:]], axis=0)
-
-
-def unpack_misc(misc):
-    film = jnp.concatenate([misc[0:4], misc[4:8]], axis=1)
-    tail = jnp.concatenate([misc[8:12], misc[12:16]], axis=1)
-    return film, tail[:, :TABLE], tail[:, TABLE:TAIL]
-
-
-def pack_attn_head(attn, head):
-    both = jnp.concatenate([*attn, head], axis=-1)
-    return jnp.pad(both, [(0, 0)] * (both.ndim - 1) + [(0, 1280 - both.shape[-1])])
+def adam_kernel(count_ref, totals, gexpand, gproject, gtaps, gmisc, gone, gtwo, *refs):
+    states = [refs[3 * i : 3 * i + 3] for i in range(6)]
+    loss_ref, norm_ref = refs[18:20]
+    outs = [refs[20 + 3 * i : 23 + 3 * i] for i in range(6)]
+
+    def total(line):
+        return jnp.sum(totals[line : line + 1, :], axis=(0, 1), keepdims=True)
+
+    scored = 0.5 * total(1)
+    norm = jnp.sqrt(total(2)) / scored
+    factor = jnp.minimum(1.0, CLIP_NORM / norm) / scored
+    loss_ref[0] = (0.5 * total(0) / scored)[0, 0]
+    norm_ref[0] = norm[0, 0]
+    steps = jnp.full((1, 1), count_ref[0], jnp.int32).astype(f32)
+    z = steps * math.log(BETA_TWO)
+    grown_two = -z * (1.0 + z / 2.0 * (1.0 + z / 3.0 * (1.0 + z / 4.0 * (1.0 + z / 5.0))))
+    grown_one = 1.0 - jnp.exp(steps * math.log(BETA_ONE))
+
+    def update(group, index, grad):
+        master, first, second = (ref[index] for ref in states[group])
+        grad = grad * factor
+        first = BETA_ONE * first + (1.0 - BETA_ONE) * grad
+        second = BETA_TWO * second + (1.0 - BETA_TWO) * grad * grad
+        step = first / grown_one / (jnp.sqrt(second / grown_two) + ADAM_EPS) + DECAY * master
+        outs[group][0][index] = master - RATES[group] * step
+        outs[group][1][index] = first
+        outs[group][2][index] = second
+
+    every = slice(None)
+    update(0, (every, slice(0, D)), gexpand[...])
+    update(0, (every, slice(D, 2 * D)), gproject[...])
+    taps = jnp.concatenate([gtaps[...], jnp.zeros((112, 128), f32)], axis=0).T
+    update(0, (every, slice(2 * D, 2 * D + 9)), taps[0:24, 0:9])
+    for i in range(3):
+        update(1, (every, slice(D * i, D * i + D)), gmisc[4 * i : 4 * i + 4, :])
+    update(1, (every, slice(3 * D, 2 * D + TABLE)), gmisc[12:16, 0:SMALL_AT])
+    update(2, (every, every), gmisc[12:16, SMALL_AT : SMALL_AT + 11])
+    for j in range(4):
+        update(3, j, gone[:, 128 * j : 128 * j + 128])
+    for j in range(2):
+        update(4, j, gtwo[:, 512 * j : 512 * j + 512])
+    for k in range(DIMS):
+        update(5, k, gone[:, 512 + 64 * k : 576 + 64 * k])
+
+
+def adam(step_count, totals, grads, states):
+    smem = pl.BlockSpec(memory_space=pltpu.SMEM)
+    one = jax.ShapeDtypeStruct((1,), f32)
+    return pl.pallas_call(
+        adam_kernel,
+        out_shape=[one, one] + [jax.ShapeDtypeStruct(s.shape, f32) for s in states],
+        in_specs=[smem] + [INVMEM] * (1 + len(grads) + len(states)),
+        out_specs=[smem, smem] + [INVMEM] * len(states),
+    )(step_count, totals, *grads, *states)
 
 
 def per_device(
@@ -1170,21 +1309,14 @@
     attn_w, attn_m1, attn_m2, mlp_w, mlp_m1, mlp_m2, head_w, head_m1, head_m2,
 ):
     core, high = lax.axis_index("mp_1"), lax.axis_index("mp_0")
-    conv_t = conv_w.T.astype(bf16)
-    cond_t = cond_w.T.astype(bf16)
-    attn_l = attn_w.astype(bf16)
-    shards = (
-        conv_t[:, :D],
-        conv_t[:, D : 2 * D],
-        jnp.pad(conv_w[2 * D :].astype(bf16), ((0, 7), (0, 104))),
-        pack_misc(cond_t[:, : 2 * D], cond_t[:, 2 * D :], small_w.T.astype(bf16)),
-        pack_attn_head([attn_l[j] for j in range(4)], head_w.astype(bf16).reshape(16, DIMS * 64)),
-        jnp.moveaxis(mlp_w.astype(bf16), 0, 1).reshape(16, 1024),
+    states = [
+        *[v.T for v in (conv_w, conv_m1, conv_m2, cond_w, cond_m1, cond_m2, small_w, small_m1, small_m2)],
+        *(attn_w, attn_m1, attn_m2, mlp_w, mlp_m1, mlp_m2),
+        *[v.transpose(1, 0, 2) for v in (head_w, head_m1, head_m2)],
+    ]
+    cam2, cells, project, taps, misc_all, one_all, two_all, pre, deep, part = forward(
+        frames, camera_ids, states[0::3], GATHER, 1
     )
-    image = jnp.arange(PAIR)
-    cam = jnp.where(image // IMAGES == core, jnp.tile(camera_ids, 2), 0)
-    cam = jnp.broadcast_to(cam[:, None], (PAIR, 128))
-    cam2, cells, project, taps, misc_all, one_all, two_all, pre, deep, part = forward((frames, cam), shards, GATHER, 1)
     instr = jnp.repeat(lax.dynamic_slice_in_dim(instruction_ids, high * 4, 4), FRAMES)
     bins = jnp.pad(
         lax.dynamic_slice_in_dim(action_bins, high * PAIR, PAIR), ((0, 0), (0, 128 - DIMS)), constant_values=-1
@@ -1203,33 +1335,13 @@
         jnp.broadcast_to(mask[:, None], (PAIR, 128)),
     )
     parts = [
-        g.reshape(*lead(dims), *s.shape)
-        for g, s, (dims, _) in zip((dmisc, done_one, done_two), shards[3:], SCATTER[3:])
+        g.reshape(*lead(dims), *slab)
+        for g, slab, (dims, _) in zip((dmisc, done_one, done_two), SLABS[3:], SCATTER[3:])
     ]
-    totals, gexpand, gproject, gtaps, gmisc, gone, gtwo = backward(
-        cells, dcells, project, taps, pre, deep, stats, parts, [s.shape for s in shards], SCATTER, 2
-    )
-    gfilm, gtable, gsmall = unpack_misc(gmisc)
-    grads = (
-        jnp.concatenate([gexpand.T, gproject.T, gtaps[:9, :24]], 0),
-        jnp.concatenate([gfilm, gtable], 1).T,
-        gsmall.T,
-        jnp.stack([gone[:, 128 * j : 128 * j + 128] for j in range(4)]),
-        jnp.moveaxis(gtwo.reshape(16, 2, 512), 1, 0),
-        gone[:, 512 : 512 + DIMS * 64].reshape(16, DIMS, 64),
-    )
-    loss_sum, count, square = (jnp.sum(totals[8 * i : 8 * i + 8]) for i in range(3))
-    loss_sum, count = 0.5 * loss_sum, 0.5 * count
-    norm = jnp.sqrt(square) / count
-    factor = jnp.minimum(1.0, CLIP_NORM / norm) / count
-    steps_done = step_count[0].astype(f32)
-    masters = (conv_w, cond_w, small_w, attn_w, mlp_w, head_w)
-    firsts = (conv_m1, cond_m1, small_m1, attn_m1, mlp_m1, head_m1)
-    seconds = (conv_m2, cond_m2, small_m2, attn_m2, mlp_m2, head_m2)
-    outs = [loss_sum / count, norm]
-    for idx in range(6):
-        outs.extend(adam(masters[idx], firsts[idx], seconds[idx], grads[idx] * factor, steps_done, RATES[idx]))
-    return tuple(outs)
+    totals, *grads = backward(cells, dcells, project, taps, pre, deep, stats, parts, SLABS, SCATTER, 2)
+    loss, norm, *new = adam(step_count, totals, grads, states)
+    new = [v.T for v in new[:9]] + new[9:15] + [v.transpose(1, 0, 2) for v in new[15:]]
+    return loss.reshape(()), norm.reshape(()), *new
 
 
 def solution(mesh):

time: 276 us -> 210 us (0.76); the launches traced: 272 us -> 210 us
  Pallas kernels: 242 us -> 205 us
  other arithmetic: 11.5 us -> 0.73 us
  local copies, waits for them, and re-layouts: 11.3 us -> 3.01 us
  between operations: 7.05 us -> 1.53 us
    pallas_call x1, Pallas kernels: 87.1 us -> 43.5 us  [middle(): pl.pallas_call(middle_kernel, out_shape=[jax.ShapeDtypeStruct((PIX * PAIR...]
    pallas_call x1, Pallas kernels: 67.5 us -> 75 us  [forward(): pl.pallas_call(functools.partial(forward_kernel, plan), out_shape=[shape(...]
    pallas_call x1, Pallas kernels: 87.4 us -> 83.4 us  [backward(): pl.pallas_call(functools.partial(backward_kernel, plan), out_shape=[shape...]
    sub x6 -> x0, other arithmetic: 3.65 us -> none  [adam(): master - rate * (m_hat / (jnp.sqrt(v_hat) + ADAM_EPS) + DECAY * master)]
    unnamed x59 -> x3, local copies, waits for them, and re-layouts: 3.33 us -> 0.1 us
    convert_element_type x4 -> x0, other arithmetic: 3.12 us -> none  [the longest x1 0.9 us: per_device(): head_w.astype(bf16).reshape(16, DIMS * 64)]
where the time goes in v2:
time: 210 us
  Pallas kernels  205 us (98%)
  local copies, waits for them, and re-layouts  3.01 us (1%)
    pallas_call x1, Pallas kernels, backward(): pl.pallas_call(functools.partial(backward_kernel, plan), out_shape=[shape...  83.4 us
    pallas_call x1, Pallas kernels, forward(): pl.pallas_call(functools.partial(forward_kernel, plan), out_shape=[shape(...  75 us
    pallas_call x1, Pallas kernels, middle(): pl.pallas_call(middle_kernel, out_shape=[jax.ShapeDtypeStruct((PIX * PAIR...  43.5 us

profile of v2, /device:TPU:1, one launch (start us, length us, event | category | flops | bytes accessed | tf_op | source)
XLA Modules:
  0.0 209.9 jit_solution(13941465075214859813)
XLA Ops:
  0.7 0.0 copy-start
  0.7 75.0 %shard_map.383 = (s32[2,24,128]{2,1,0:T(8,128)}, bf16[1944,512]{1,0:T(8,128)(2,1)}, bf16[4,2,4,2,24,512]{5,4,3,2,1,0:T(8,128)(2,1)}, f32[4,16,384]{2,1,0:T(8,128...) custom-call(bf16[12,81,512]{2,1,0:T(8,128)(2,1)} %refs_0_.1, ...), custom_call_target="tpu_custom_call" | custom-call | tf_op jit(solution)/shard_map/pallas_call | solution.py:904
  75.7 0.0 copy-done
  75.7 0.1 constant_dynamic-slice_fusion
  75.8 0.1 copy.45
  75.8 0.6 pad.4.bins
  76.4 0.7 dynamic-slice_convert_fusion
  77.2 0.7 broadcast_in_dim.23.mask
  77.8 0.7 dynamic_slice.9
  78.6 0.1 broadcast_in_dim.20
  78.7 0.1 broadcast_in_dim.21
  78.7 0.7 broadcast_in_dim.22.instr
  79.4 43.5 %shard_map.384 = (bf16[1944,512]{1,0:T(8,128)(2,1)}, bf16[1024,512]{1,0:T(8,128)(2,1)}, bf16[2,512,1280]{2,1,0:T(8,128)(2,1)}, bf16[2,512,1024]{2,1,0:T(8,128)(2,1)}, f32[16,128]{1,0:T(8,128)}) custom-call(s32[1]{0:T(128)} %bitcast.4.core_ref, f32[1944,512]{1,0:T(8,128)} %get-tuple-element.63.part, bf16[1944,512]{1,0:T(8,128)(2,1)} %get-tuple-element.62.cells.refs_0_, ...), custom_call_target="tpu_custom_call" | custom-call | tf_op jit(solution)/shard_map/pallas_call | solution.py:674
  122.9 83.4 %shard_map.385 = (f32[8,128]{1,0:T(8,128)}, f32[24,512]{1,0:T(8,128)}, f32[24,512]{1,0:T(8,128)}, f32[16,128]{1,0:T(8,128)}, f32[16,512]{1,0:T(8,128)}, /*index=5*/f32[16,1280]{1,0:T(8,128)}, f32[16,1024]{1,0:T(8,128)}) custom-call(bf16[1944,512]{1,0:T(8,128)(2,1)} %get-tuple-element.62.cells.refs_0_, bf16[1944,512]{1,0:T(8,128)(2,1)} %get-tuple-element.68.refs_1_, ...), custom_call_target="tpu_custom_call" | custom-call | tf_op jit(solution)/shard_map/pallas_call | solution.py:1203
  207.0 2.7 %shard_map.386 = (f32[1]{0:T(128)}, f32[1]{0:T(128)}, f32[24,1033]{1,0:T(8,128)}, f32[24,1033]{1,0:T(8,128)}, f32[24,1033]{1,0:T(8,128)}, /*index=5*/f32[4,1770]...) custom-call(s32[1]{0:T(128)S(6)} %copy.46.count_ref, ...), custom_call_target="tpu_custom_call" | custom-call | tf_op jit(solution)/shard_map/pallas_call | solution.py:1298
Async XLA Ops:
  0.7 75.0 %copy-start = (s32[48,11]{0,1:T(8,128)S(1)}, s32[48,11]{0,1:T(8,128)}, u32[]{:S(2)}) copy-start(s32[48,11]{0,1:T(8,128)} %param.27) | copy-start | bytes 6340
